TPU v7x, 512 devices: a whole 4x4x16 slice. The times are simulated.
512 devices in a mesh: dp: 128 (over y, z, core), panel: 4 (over x).
Axes of the slice: x: 4, y: 4, z: 16, core: 2. Of those that a mesh axis runs over, the one named last changes fastest.
Arguments:
- sample: float32 [32768, 4096], P('dp'), may hold values from -80 to 80
- start_basis: float32 [4096, 512], P('dp', 'panel'), may hold values from -6 to 6
- corpus: float32 [12288, 4096], P('dp'), may hold values from -16 to 16
- owner_shard: int32 [12288, 1], P('dp'), may hold values from 0 to 127; in each aligned block of 96 rows (0 to 95, 96 to 191, ...) at most 2 rows name the same one
Outputs:
- routed: float32 [32768, 512], P('dp', 'panel')
Inputs may be any that keep to these rules, and one draw needn't show every extreme that they name: Among the 96 rows of one device at most 2 have the same owner_shard, and in some device exactly 2 do.
All inputs are finite; a program needn't handle non-finite values.
Results may differ from a plain program's by a relative error of at most 0.0003.
Values sent between devices are 32-bit elements; how exact they have to be, the bound alone decides.
No kernel may reach another device: no remote copies, remote signals or barrier semaphores. Data moves between devices by JAX's collectives and lax.ppermute only.
A program may use at most 64 MiB of HBM per device.

v0:
```python
import functools

import jax
import jax.numpy as jnp
from jax import lax
from jax.experimental import pallas as pl
from jax.experimental.pallas import tpu as pltpu
from jax.sharding import Mesh
from jax.sharding import PartitionSpec as P

DP = ("y", "z", "core")
HIGHEST = lax.Precision.HIGHEST
HIGH = lax.Precision.HIGH


def swap(parts, axis):
    return lax.all_to_all(parts, axis, 0, 0, tiled=True)


def spread(block, axis):
    return swap(jnp.broadcast_to(block[None], (lax.axis_size(axis), *block.shape)), axis)


def pack(*pieces):
    count = pieces[0].shape[0]
    rows = sum(piece.shape[1] for piece in pieces)
    fill = -rows % 8
    if fill:
        pieces += (jnp.zeros((count, fill, pieces[0].shape[2]), jnp.float32),)
    return jnp.concatenate(pieces, axis=1)


def share(row, count):
    return jnp.broadcast_to(row[None], (count, *row.shape))


def in_lanes(values, count, lanes):
    rows = values.reshape(count, -1, min(lanes, values.size // count))
    return jnp.pad(rows, ((0, 0), (0, 0), (0, lanes - rows.shape[2])))


def dot_t(a, b):
    return lax.dot_general(
        a, b, (((1,), (1,)), ((), ())), precision=HIGHEST, preferred_element_type=jnp.float32
    )


def invert_factor(block_ref, inverse_ref):
    n = block_ref.shape[0]
    groups = n // 8
    sub = lax.broadcasted_iota(jnp.int32, (8, n), 0)
    lane = lax.broadcasted_iota(jnp.int32, (8, n), 1)

    def full(x):
        return jnp.broadcast_to(x, (8, n))

    left = [block_ref[8 * g : 8 * g + 8, :] for g in range(groups)]
    right = [(lane == sub + 8 * g).astype(jnp.float32) for g in range(groups)]
    for b in range(groups):
        at = 8 * b
        columns = [full(left[b][:, at + i : at + i + 1]) for i in range(8)]
        pivot = [[full(columns[i][j : j + 1, :]) for i in range(j + 1)] for j in range(8)]
        rows = [full(left[b][j : j + 1, :]) for j in range(8)]
        inverse = [full(right[b][j : j + 1, :]) for j in range(8)]
        below = [
            [full(left[g][:, at + i : at + i + 1]) for i in range(8)]
            for g in range(b + 1, groups)
        ]
        scale = []
        for i in range(8):
            scale.append(1.0 / pivot[i][i])
            for j in range(i + 1, 8):
                factor = pivot[j][i] * scale[i]
                for k in range(i + 1, j + 1):
                    pivot[j][k] = pivot[j][k] - factor * pivot[k][i]
                rows[j] = rows[j] - factor * rows[i]
                inverse[j] = inverse[j] - factor * inverse[i]
        for g in range(b + 1, groups):
            column = below[g - b - 1]
            for i in range(8):
                factor = column[i] * scale[i]
                for k in range(i + 1, 8):
                    column[k] = column[k] - factor * pivot[k][i]
                left[g] = left[g] - factor * rows[i]
                right[g] = right[g] - factor * inverse[i]
        done, diagonal = inverse[0], pivot[0][0]
        for j in range(1, 8):
            done = jnp.where(sub == j, inverse[j], done)
            diagonal = jnp.where(sub == j, pivot[j][j], diagonal)
        inverse_ref[at : at + 8, :] = done * lax.rsqrt(diagonal)


def solve_kernel(panel_ref, stacked_ref, out_ref, work_ref, inverse_ref):
    blocks, _, w = work_ref.shape
    kept = out_ref.shape[0]
    work_ref[...] = stacked_ref[...]

    def finish(k):
        solved = dot_t(work_ref[k, (k + 1) * w :, :], inverse_ref[...])
        for m in range(k + 1, blocks):
            at = (m - k - 1) * w
            work_ref[m, m * w :, :] -= dot_t(solved[at:], solved[at : at + w])

        @pl.when(panel_ref[0] == k)
        def _():
            out_ref[...] = solved[-kept:]

    def step(k, carry):
        invert_factor(work_ref.at[k, pl.ds(pl.multiple_of(k * w, w), w)], inverse_ref)
        for q in range(blocks):
            pl.when(k == q)(functools.partial(finish, q))
        return carry

    lax.fori_loop(0, blocks, step, 0)


def solve_rows(panel, stacked, kept):
    blocks, height, w = stacked.shape
    vmem = pl.BlockSpec(memory_space=pltpu.VMEM)
    return pl.pallas_call(
        solve_kernel,
        out_shape=jax.ShapeDtypeStruct((kept, w), jnp.float32),
        in_specs=[pl.BlockSpec(memory_space=pltpu.SMEM), vmem],
        out_specs=vmem,
        scratch_shapes=[
            pltpu.VMEM((blocks, height, w), jnp.float32),
            pltpu.VMEM((w, w), jnp.float32),
        ],
        compiler_params=pltpu.CompilerParams(vmem_limit_bytes=32 << 20),
        cost_estimate=pl.CostEstimate(
            flops=4 * blocks * height * blocks * w * w, bytes_accessed=8 * stacked.size, transcendentals=0
        ),
    )(panel, stacked)


def body(sample, start_basis, corpus, owner_shard):
    ny, nz, nc, np_ = (lax.axis_size(name) for name in (*DP, "panel"))
    owners = ny * nz * nc
    slab, width = start_basis.shape
    depth = slab * owners
    directions = width * np_
    total_rows = sample.shape[0] * owners

    basis = spread(spread(spread(start_basis, "z"), "y"), "core")
    basis = basis.transpose(1, 2, 0, 3, 4).reshape(depth, width)

    column_sums = jnp.sum(sample, axis=0)
    projected = jnp.dot(sample, basis, precision=HIGH)
    lifted = jnp.sum(projected, axis=0, keepdims=True)
    cross = lax.dot_general(sample, projected, (((0,), (0,)), ((), ())), precision=HIGH)

    for axis, count in (("core", nc), ("y", ny), ("z", nz)):
        message = pack(
            cross.reshape(count, -1, width),
            in_lanes(column_sums, count, width),
            share(lifted, count),
        )
        rows = cross.shape[0] // count
        sums = jnp.sum(swap(message, axis), axis=0)
        mean_rows = -(-rows // width)
        cross = sums[:rows]
        column_sums = sums[rows : rows + mean_rows].reshape(-1)[:rows]
        lifted = sums[rows + mean_rows : rows + mean_rows + 1]
    mean = column_sums / total_rows
    image = cross / total_rows - mean[:, None] * (lifted / total_rows)

    image_rows = spread(image, "panel").transpose(1, 0, 2).reshape(slab, directions)
    gram = lax.dot_general(image_rows, image, (((0,), (0,)), ((), ())), precision=HIGHEST)

    rest = directions // owners
    part = directions // nz
    got = swap(
        pack(
            share(image, nz),
            in_lanes(share(mean, nz), nz, width),
            gram.reshape(nz, part, width),
        ),
        "z",
    )
    image = got[:, :slab].reshape(-1, width)
    mean = got[:, slab, :slab].reshape(-1)
    gram = jnp.sum(got[:, slab + 1 : slab + 1 + part], axis=0)
    for axis in ("y", "core"):
        rows = image.shape[0]
        mean_rows = rows // width
        got = spread(
            pack(image[None], in_lanes(mean[None], 1, width), gram[None])[0], axis
        )
        image = got[:, :rows].reshape(-1, width)
        mean = got[:, rows : rows + mean_rows].reshape(-1)
        gram = jnp.sum(got[:, rows + mean_rows : rows + mean_rows + part], axis=0)

    y_index, core_index = lax.axis_index("y"), lax.axis_index("core")
    reduced = jnp.dot(corpus - mean[None, :], image, precision=HIGH)
    corpus_rows = corpus.shape[0]
    capacity = max(2, 2 * corpus_rows // owners)
    owner_ids = owner_shard[:, 0]
    choose = (owner_ids[:, None] == jnp.arange(owners, dtype=jnp.int32)[None, :]).astype(jnp.int32)
    running = jnp.cumsum(choose, axis=0)
    slot_index = jnp.sum(running * choose, axis=1) - 1
    target = owner_ids * capacity + slot_index
    slot_range = jnp.arange(owners * capacity, dtype=jnp.int32)
    placing = (target[None, :] == slot_range[:, None]).astype(jnp.float32)
    outgoing = jnp.dot(placing, reduced, precision=HIGHEST).reshape(owners, capacity, width)

    own_gram = lax.dynamic_slice_in_dim(gram, (y_index * nc + core_index) * rest, rest, 0)
    got = swap(jnp.concatenate([outgoing, share(own_gram, owners)], axis=1), DP)
    routed = got[:, :capacity].reshape(owners * capacity, width)
    gram = got[:, capacity:].reshape(ny, nz, nc, rest, width).transpose(1, 0, 2, 3, 4)
    gram = gram.reshape(directions, width)

    stacked = spread(jnp.concatenate([gram, routed], axis=0), "panel")
    panel = lax.axis_index("panel").astype(jnp.int32).reshape(1)
    return solve_rows(panel, stacked, owners * capacity)


def solution(mesh):
    y, z, core, panel = 4, 16, 2, mesh.shape["panel"]
    fine = Mesh(mesh.devices.reshape(y, z, core, panel), (*DP, "panel"))
    placed = (P(DP, None), P(DP, "panel"), P(DP, None), P(DP, None))
    return jax.shard_map(
        body, mesh=fine, in_specs=placed, out_specs=P(DP, "panel"), check_vma=False
    )
```

profile of v0, /device:TPU:1, one launch (start us, length us, event | category | flops | bytes accessed | tf_op | source)
XLA Modules:
  0.0 292.0 jit_solution(12531282400620832450)
XLA Ops:
  0.0 0.7 broadcast_in_dim.46
  0.7 28.7 %all_to_all.60 = f32[16,32,128]{2,1,0:T(8,128)S(1)} all-to-all(f32[16,32,128]{2,1,0:T(8,128)S(1)} %broadcast_in_dim.46), channel_id=1, replica_groups=mesh['y'=4,'z'=16,'core'=2,'panel'=4] {'z'}, dimensions={0} | all-to-all | bytes 524288 | tf_op jit(solution)/shard_map/all_to_all | solution.py:17
  29.4 1.1 broadcast_in_dim.47
  30.5 4.2 %all-to-all-start.1 = ((f32[4,16,32,128]{3,2,1,0:T(8,128)}), f32[4,16,32,128]{3,2,1,0:T(8,128)S(1)}, u32[]{:S(2)}, u32[]{:S(2)}) async-start(f32[4,16,32,128]{3,2,1,0:T(8,128)} %broadcast_in_dim.47), calls=%async_computation.1 | async-start | bytes 2097152 | tf_op jit(solution)/shard_map/all_to_all | solution.py:17
  34.7 2.4 reduce_sum.82
  37.2 7.3 %all-to-all-done.1 = f32[4,16,32,128]{3,2,1,0:T(8,128)S(1)} async-done(((f32[4,16,32,128]{3,2,1,0:T(8,128)}), f32[4,16,32,128]{3,2,1,0:T(8,128)S(1)}, u32[]{:S(2)}, u32[]{:S(2)}) %all-to-all-start.1) | async-done | bytes 1048608 | tf_op jit(solution)/shard_map/all_to_all | solution.py:17
  44.5 0.2 broadcast_in_dim.48
  44.7 12.7 %all_to_all.61 = f32[2,4,16,32,128]{4,3,2,1,0:T(8,128)S(1)} all-to-all(f32[2,4,16,32,128]{4,3,2,1,0:T(8,128)S(1)} %broadcast_in_dim.48), channel_id=1, replica_groups=mesh['y'=4,'z'=16,'core'=2,'panel'=4] {'core'}, dimensions={0} | all-to-all | bytes 4194304 | tf_op jit(solution)/shard_map/all_to_all | solution.py:17
  57.4 0.2 copy.47
  57.6 2.0 copy-done
  59.6 1.9 fusion.15
  61.4 1.6 convolution_bitcast_fusion
  63.0 1.9 copy.59
  64.9 4.1 %concatenate.24 = f32[2,2072,128]{2,1,0:T(8,128)S(1)} concatenate(f32[2,2048,128]{2,1,0:T(8,128)} %bitcast.59, f32[2,16,128]{2,1,0:T(8,128)S(1)} %bitcast.70, f32[2,1,128]{2,1,0:T(1,128)S(1)} %broadcast_in_dim.49, f32[2,7,128]{2,1,0:T(8,128)S(1)} %broadcast_in_dim.50), dimensions={1} | concatenate | bytes 4243456 | tf_op jit(solution)/shard_map/concatenate | solution.py:30
  69.0 6.3 %all_to_all.62 = f32[2,2072,128]{2,1,0:T(8,128)} all-to-all(f32[2,2072,128]{2,1,0:T(8,128)S(1)} %concatenate.24), channel_id=1, replica_groups=mesh['y'=4,'z'=16,'core'=2,'panel'=4] {'core'}, dimensions={0} | all-to-all | bytes 4243456 | tf_op jit(solution)/shard_map/all_to_all | solution.py:17
  75.3 1.9 reduce_sum.84
  77.2 1.1 maximum_maximum_fusion
  78.4 3.5 %all-to-all-start.4 = ((f32[4,520,128]{2,1,0:T(8,128)}), f32[4,520,128]{2,1,0:T(8,128)S(1)}, u32[]{:S(2)}, u32[]{:S(2)}) async-start(f32[4,520,128]{2,1,0:T(8,128)} %maximum_maximum_fusion), calls=%async_computation.4 | async-start | bytes 2129920 | tf_op jit(solution)/shard_map/all_to_all | solution.py:17
  82.0 14.9 %all-to-all-done.4 = f32[4,520,128]{2,1,0:T(8,128)S(1)} async-done(((f32[4,520,128]{2,1,0:T(8,128)}), f32[4,520,128]{2,1,0:T(8,128)S(1)}, u32[]{:S(2)}, u32[]{:S(2)}) %all-to-all-start.4) | async-done | bytes 1064992 | tf_op jit(solution)/shard_map/all_to_all | solution.py:17
  97.1 0.1 fusion.4
  97.2 23.7 %all_to_all.63 = f32[16,40,128]{2,1,0:T(8,128)S(1)} all-to-all(f32[16,40,128]{2,1,0:T(8,128)S(1)} %fusion.4), channel_id=1, replica_groups=mesh['y'=4,'z'=16,'core'=2,'panel'=4] {'z'}, dimensions={0} | all-to-all | bytes 655360 | tf_op jit(solution)/shard_map/all_to_all | solution.py:17
  121.0 0.6 broadcast_in_dim.58
  121.7 4.0 %all-to-all-start.6 = ((f32[4,32,128]{2,1,0:T(8,128)}), f32[4,32,128]{2,1,0:T(8,128)S(1)}, u32[]{:S(2)}, u32[]{:S(2)}) async-start(f32[4,32,128]{2,1,0:T(8,128)} %broadcast_in_dim.58), calls=%async_computation.6 | async-start | bytes 131072 | tf_op jit(solution)/shard_map/all_to_all | solution.py:17
  125.8 4.4 %all-to-all-done.6 = f32[4,32,128]{2,1,0:T(8,128)S(1)} async-done(((f32[4,32,128]{2,1,0:T(8,128)}), f32[4,32,128]{2,1,0:T(8,128)S(1)}, u32[]{:S(2)}, u32[]{:S(2)}) %all-to-all-start.6) | async-done | bytes 65568 | tf_op jit(solution)/shard_map/all_to_all | solution.py:17
  130.2 0.1 copy.57
  130.3 0.4 fusion.10
  130.7 0.9 maximum_maximum_fusion.1
  131.6 12.6 %all-to-all-start.7 = ((f32[16,72,128]{2,1,0:T(8,128)}), f32[16,72,128]{2,1,0:T(8,128)S(1)}, u32[]{:S(2)}, u32[]{:S(2)}) async-start(f32[16,72,128]{2,1,0:T(8,128)} %maximum_maximum_fusion.1), calls=%async_computation.7 | async-start | bytes 1179648 | tf_op jit(solution)/shard_map/all_to_all | solution.py:17
  144.3 24.5 %all-to-all-done.7 = f32[16,72,128]{2,1,0:T(8,128)S(1)} async-done(((f32[16,72,128]{2,1,0:T(8,128)}), f32[16,72,128]{2,1,0:T(8,128)S(1)}, u32[]{:S(2)}, u32[]{:S(2)}) %all-to-all-start.7) | async-done | bytes 589856 | tf_op jit(solution)/shard_map/all_to_all | solution.py:17
  168.8 0.1 reshape_broadcast_in_dim_reshape_squeeze.3
  168.9 0.1 maximum_bitcast_fusion.1
  169.1 1.1 broadcast_in_dim.123
  170.2 3.5 %all-to-all-start.8 = ((f32[4,552,128]{2,1,0:T(8,128)}), f32[4,552,128]{2,1,0:T(8,128)S(1)}, u32[]{:S(2)}, u32[]{:S(2)}) async-start(f32[4,552,128]{2,1,0:T(8,128)} %broadcast_in_dim.123), calls=%async_computation.8 | async-start | bytes 2260992 | tf_op jit(solution)/shard_map/all_to_all | solution.py:17
  173.8 0.1 reduce_window_sum.11
  173.9 0.2 select_reduce_fusion
  174.1 9.7 %all-to-all-done.8 = f32[4,552,128]{2,1,0:T(8,128)S(1)} async-done(((f32[4,552,128]{2,1,0:T(8,128)}), f32[4,552,128]{2,1,0:T(8,128)S(1)}, u32[]{:S(2)}, u32[]{:S(2)}) %all-to-all-start.8) | async-done | bytes 1130528 | tf_op jit(solution)/shard_map/all_to_all | solution.py:17
  184.0 0.1 broadcast_in_dim.126
  184.2 13.1 %all_to_all.64 = f32[2,2096,128]{2,1,0:T(8,128)S(1)} all-to-all(f32[2,2096,128]{2,1,0:T(8,128)S(1)} %broadcast_in_dim.126), channel_id=1, replica_groups=mesh['y'=4,'z'=16,'core'=2,'panel'=4] {'core'}, dimensions={0} | all-to-all | bytes 4292608 | tf_op jit(solution)/shard_map/all_to_all | solution.py:17
  197.3 0.1 slice.99
  197.4 1.3 copy-done.1
  198.7 1.1 fusion
  199.8 0.2 fusion.6
  200.0 0.1 pad_maximum_fusion
  200.1 47.2 %all_to_all.65 = f32[128,6,128]{2,1,0:T(8,128)S(1)} all-to-all(f32[128,6,128]{2,1,0:T(8,128)S(1)} %pad_maximum_fusion), channel_id=1, replica_groups=mesh['y'=4,'z'=16,'core'=2,'panel'=4] {'y','z','core'}, dimensions={0} | all-to-all | bytes 786432 | tf_op jit(solution)/shard_map/all_to_all | solution.py:17
  247.5 1.3 broadcast_in_dim.128
  248.8 3.7 %all-to-all-start.11 = ((f32[4,768,128]{2,1,0:T(8,128)}), f32[4,768,128]{2,1,0:T(8,128)S(1)}, u32[]{:S(2)}, u32[]{:S(2)}) async-start(f32[4,768,128]{2,1,0:T(8,128)} %broadcast_in_dim.128), calls=%async_computation.11 | async-start | bytes 3145728 | tf_op jit(solution)/shard_map/all_to_all | solution.py:17
  252.6 19.3 %all-to-all-done.11.stacked_ref = f32[4,768,128]{2,1,0:T(8,128)S(1)} async-done(((f32[4,768,128]{2,1,0:T(8,128)}), f32[4,768,128]{2,1,0:T(8,128)S(1)}, u32[]{:S(2)}, u32[]{:S(2)}) %all-to-all-start.11) | async-done | bytes 1572896 | tf_op jit(solution)/shard_map/all_to_all | solution.py:17
  271.9 20.2 %shard_map.46 = f32[256,128]{1,0:T(8,128)} custom-call(s32[1]{0:T(128)} %bitcast.panel_ref, f32[4,768,128]{2,1,0:T(8,128)S(1)} %all-to-all-done.11.stacked_ref), custom_call_target="tpu_custom_call" | custom-call | flops 805306368 | bytes 3145728 | tf_op jit(solution)/shard_map/pallas_call | solution.py:120
  (48 shorter events, 1.2 us)
Async XLA Ops:
  30.5 13.9 %all-to-all-start.1 = ((f32[4,16,32,128]{3,2,1,0:T(8,128)}), f32[4,16,32,128]{3,2,1,0:T(8,128)S(1)}, u32[]{:S(2)}, u32[]{:S(2)}) async-start(f32[4,16,32,128]{3,2,1,0:T(8,128)} %broadcast_in_dim.47), calls=%async_computation.1 | async-start | bytes 2097152 | tf_op jit(solution)/shard_map/all_to_all | solution.py:17
  57.4 2.2 copy-start
  78.4 18.5 %all-to-all-start.4 = ((f32[4,520,128]{2,1,0:T(8,128)}), f32[4,520,128]{2,1,0:T(8,128)S(1)}, u32[]{:S(2)}, u32[]{:S(2)}) async-start(f32[4,520,128]{2,1,0:T(8,128)} %maximum_maximum_fusion), calls=%async_computation.4 | async-start | bytes 2129920 | tf_op jit(solution)/shard_map/all_to_all | solution.py:17
  121.7 8.5 %all-to-all-start.6 = ((f32[4,32,128]{2,1,0:T(8,128)}), f32[4,32,128]{2,1,0:T(8,128)S(1)}, u32[]{:S(2)}, u32[]{:S(2)}) async-start(f32[4,32,128]{2,1,0:T(8,128)} %broadcast_in_dim.58), calls=%async_computation.6 | async-start | bytes 131072 | tf_op jit(solution)/shard_map/all_to_all | solution.py:17
  131.6 37.2 %all-to-all-start.7 = ((f32[16,72,128]{2,1,0:T(8,128)}), f32[16,72,128]{2,1,0:T(8,128)S(1)}, u32[]{:S(2)}, u32[]{:S(2)}) async-start(f32[16,72,128]{2,1,0:T(8,128)} %maximum_maximum_fusion.1), calls=%async_computation.7 | async-start | bytes 1179648 | tf_op jit(solution)/shard_map/all_to_all | solution.py:17
  169.1 4.6 %copy-start.2 = (s32[96,1]{0,1:T(1,128)S(1)}, s32[96,1]{0,1:T(1,128)}, u32[]{:S(2)}) copy-start(s32[96,1]{0,1:T(1,128)} %param.7) | copy-start | bytes 1156
  170.2 13.7 %all-to-all-start.8 = ((f32[4,552,128]{2,1,0:T(8,128)}), f32[4,552,128]{2,1,0:T(8,128)S(1)}, u32[]{:S(2)}, u32[]{:S(2)}) async-start(f32[4,552,128]{2,1,0:T(8,128)} %broadcast_in_dim.123), calls=%async_computation.8 | async-start | bytes 2260992 | tf_op jit(solution)/shard_map/all_to_all | solution.py:17
  197.3 1.4 copy-start.1
  248.8 23.1 %all-to-all-start.11 = ((f32[4,768,128]{2,1,0:T(8,128)}), f32[4,768,128]{2,1,0:T(8,128)S(1)}, u32[]{:S(2)}, u32[]{:S(2)}) async-start(f32[4,768,128]{2,1,0:T(8,128)} %broadcast_in_dim.128), calls=%async_computation.11 | async-start | bytes 3145728 | tf_op jit(solution)/shard_map/all_to_all | solution.py:17
where the time goes:
time: 293 us; the launch traced here: 292 us
  blocking collectives  132 us (45%)
  waiting for transfers between devices  80.1 us (27%)
  starting transfers between devices  31.6 us (11%)
  Pallas kernels  20.2 us (7%)
  local copies, waits for them, and re-layouts  15.7 us (5%)
  other arithmetic  7.36 us (3%)
  matrix products  5.09 us (2%)
    all_to_all x6, blocking collectives, swap(): return lax.all_to_all(parts, axis, 0, 0, tiled=True)  132 us
    all_to_all x6, waiting for transfers between devices, swap(): return lax.all_to_all(parts, axis, 0, 0, tiled=True)  80.1 us
    all_to_all x6, starting transfers between devices, swap(): return lax.all_to_all(parts, axis, 0, 0, tiled=True)  31.6 us
    pallas_call x1, Pallas kernels, solve_rows(): pl.pallas_call(solve_kernel, out_shape=jax.ShapeDtypeStruct((kept, w), jn...  20.2 us
  transfers between devices with their start and end apart: 6, of which 6 were waited for; matrix products, arithmetic and copies ran while one was open for 1% of the time, Pallas kernels for 0%

commit v1 on v0

v1 whole, which is shorter than its diff:
```python
import functools

import jax
import jax.numpy as jnp
from jax import lax
from jax.experimental import pallas as pl
from jax.experimental.pallas import tpu as pltpu
from jax.sharding import Mesh
from jax.sharding import PartitionSpec as P

DP = ("y", "z", "core")
HIGHEST = lax.Precision.HIGHEST


def swap(parts, axis):
    return lax.all_to_all(parts, axis, 0, 0, tiled=True)


def spread(block, axis):
    return swap(jnp.broadcast_to(block[None], (lax.axis_size(axis), *block.shape)), axis)


def dot_t(a, b):
    return lax.dot_general(
        a, b, (((1,), (1,)), ((), ())), precision=HIGHEST, preferred_element_type=jnp.float32
    )


def invert_factor(block_ref, inverse_ref):
    n = block_ref.shape[0]
    groups = n // 8
    sub = lax.broadcasted_iota(jnp.int32, (8, n), 0)
    lane = lax.broadcasted_iota(jnp.int32, (8, n), 1)

    def full(x):
        return jnp.broadcast_to(x, (8, n))

    left = [block_ref[8 * g : 8 * g + 8, :] for g in range(groups)]
    right = [(lane == sub + 8 * g).astype(jnp.float32) for g in range(groups)]
    for b in range(groups):
        at = 8 * b
        columns = [full(left[b][:, at + i : at + i + 1]) for i in range(8)]
        pivot = [[full(columns[i][j : j + 1, :]) for i in range(j + 1)] for j in range(8)]
        rows = [full(left[b][j : j + 1, :]) for j in range(8)]
        inverse = [full(right[b][j : j + 1, :]) for j in range(8)]
        below = [
            [full(left[g][:, at + i : at + i + 1]) for i in range(8)]
            for g in range(b + 1, groups)
        ]
        scale = []
        for i in range(8):
            scale.append(1.0 / pivot[i][i])
            for j in range(i + 1, 8):
                factor = pivot[j][i] * scale[i]
                for k in range(i + 1, j + 1):
                    pivot[j][k] = pivot[j][k] - factor * pivot[k][i]
                rows[j] = rows[j] - factor * rows[i]
                inverse[j] = inverse[j] - factor * inverse[i]
        for g in range(b + 1, groups):
            column = below[g - b - 1]
            for i in range(8):
                factor = column[i] * scale[i]
                for k in range(i + 1, 8):
                    column[k] = column[k] - factor * pivot[k][i]
                left[g] = left[g] - factor * rows[i]
                right[g] = right[g] - factor * inverse[i]
        done, diagonal = inverse[0], pivot[0][0]
        for j in range(1, 8):
            done = jnp.where(sub == j, inverse[j], done)
            diagonal = jnp.where(sub == j, pivot[j][j], diagonal)
        inverse_ref[at : at + 8, :] = done * lax.rsqrt(diagonal)


def split(x):
    high = x.astype(jnp.bfloat16)
    return high, (x - high.astype(jnp.float32)).astype(jnp.bfloat16)


def dot_split(a, b, dims):
    (ah, al), (bh, bl) = a, b

    def dot(x, y):
        return lax.dot_general(x, y, (dims, ((), ())), preferred_element_type=jnp.float32)

    return dot(ah, bh) + (dot(ah, bl) + dot(al, bh))


def tdot(a, b):
    return lax.dot_general(
        a, b, (((0,), (0,)), ((), ())), precision=HIGHEST, preferred_element_type=jnp.float32
    )


def up8(rows):
    return -(-rows // 8) * 8


def sample_kernel(sample_ref, basis_ref, out_ref):
    rows, depth = sample_ref.shape
    cores, blocks, slab, w = basis_ref.shape
    tile = 2 * cores * slab * max(1, 128 // (cores * slab))
    per = tile // (cores * slab)
    half = depth // cores
    sums_at = half
    lifted_at = half + half // w
    projected = jnp.zeros((rows, w), jnp.float32)
    for t in range(depth // tile):
        part = jnp.concatenate(
            [basis_ref[c, t * per + i] for i in range(per) for c in range(cores)], axis=0
        )
        columns = split(sample_ref[:, t * tile : (t + 1) * tile])
        projected += dot_split(columns, split(part), ((1,), (0,)))
    lifted = jnp.sum(projected, axis=0, keepdims=True)
    pieces = split(projected)
    for t in range(depth // tile):
        columns = sample_ref[:, t * tile : (t + 1) * tile]
        core, at = t * tile // half, t * tile % half
        out_ref[core, at : at + tile, :] = dot_split(split(columns), pieces, ((0,), (0,)))
        sums = jnp.sum(columns, axis=0, keepdims=True)
        for q in range(tile // w):
            row = sums_at + at // w + q
            out_ref[core, row : row + 1, :] = sums[:, q * w : (q + 1) * w]
    for c in range(cores):
        out_ref[c, lifted_at:, :] = jnp.broadcast_to(lifted, (out_ref.shape[1] - lifted_at, w))


def halve_kernel(got_ref, out_ref):
    count, height, w = out_ref.shape
    rows = got_ref.shape[1]
    main = max(m for m in range(0, rows, w) if m + m // w < rows)
    got = sum(got_ref[i] for i in range(1, got_ref.shape[0])) + got_ref[0]
    lifted = got[main + main // w : main + main // w + 1]
    each, sums = main // count, main // w // count
    for i in range(count):
        out_ref[i, :each, :] = got[i * each : (i + 1) * each]
        out_ref[i, each : each + sums, :] = got[main + i * sums : main + (i + 1) * sums]
        out_ref[i, each + sums :, :] = jnp.broadcast_to(lifted, (height - each - sums, w))


def slab_kernel(slab, got_ref, out_ref):
    count, _, w = out_ref.shape
    got = sum(got_ref[i] for i in range(1, got_ref.shape[0])) + got_ref[0]
    main = slab * count
    in_row = w // slab
    lifted = got[main + main // w : main + main // w + 1]
    lane = lax.broadcasted_iota(jnp.int32, (1, w), 1) // slab
    for i in range(count):
        row = main + i // in_row
        sums = jnp.where(lane == i % in_row, got[row : row + 1], 0.0)
        out_ref[i, :slab, :] = got[i * slab : (i + 1) * slab]
        out_ref[i, slab : slab + 1, :] = sums
        out_ref[i, slab + 1 :, :] = jnp.broadcast_to(lifted, (out_ref.shape[1] - slab - 1, w))


def image_kernel(total_rows, got_ref, spread_ref, own_ref):
    copies, slab, w = spread_ref.shape
    got = sum(got_ref[i] for i in range(1, got_ref.shape[0])) + got_ref[0]
    mean = got[slab : slab + 1] / total_rows
    lifted = got[slab + 1 : slab + 2] / total_rows
    here = lax.broadcasted_iota(jnp.int32, (slab, w), 1) % slab == lax.broadcasted_iota(
        jnp.int32, (slab, w), 0
    )
    column = jnp.sum(jnp.where(here, mean, 0.0), axis=1, keepdims=True)
    image = got[:slab] / total_rows - column * lifted
    for i in range(copies):
        spread_ref[i] = image
    own_ref[:slab, :] = image
    own_ref[slab:, :] = jnp.broadcast_to(mean, (own_ref.shape[0] - slab, w))


def gram_kernel(panel_ref, images_ref, out_ref):
    panel = panel_ref[0]
    w = out_ref.shape[1]
    own, after = images_ref[panel], images_ref[(panel + 1) % 4]
    last = panel == 3
    low = panel % 2
    out_ref[:w, :] = tdot(own, own)
    out_ref[w : 2 * w, :] = tdot(jnp.where(last, own, after), jnp.where(last, after, own))
    across = tdot(images_ref[low + 2], images_ref[low])
    out_ref[2 * w :, :] = jnp.where(panel < 2, across[: w // 2], across[w // 2 :])


def join_kernel(got_ref, own_ref, out_ref):
    gram = sum(got_ref[i] for i in range(1, got_ref.shape[0])) + got_ref[0]
    top = own_ref.shape[0]
    for i in range(out_ref.shape[0]):
        out_ref[i, :top, :] = own_ref[...]
        out_ref[i, top:, :] = gram


def gather_z_kernel(slab, got_ref, out_ref):
    count, height, w = got_ref.shape
    top = slab + 8
    in_row = w // slab
    gram = sum(got_ref[i, top:, :] for i in range(1, count)) + got_ref[0, top:, :]
    main = count * slab
    for c in range(out_ref.shape[0]):
        for i in range(count):
            out_ref[c, i * slab : (i + 1) * slab, :] = got_ref[i, :slab, :]
        for r in range(count // in_row):
            mean = sum(got_ref[r * in_row + q, slab : slab + 1, :] for q in range(in_row))
            out_ref[c, main + r : main + r + 1, :] = mean
        at = out_ref.shape[1] - gram.shape[0]
        for r in range(main + count // in_row, at):
            out_ref[c, r : r + 1, :] = mean
        out_ref[c, at:, :] = gram


def gather_y_kernel(main, sums, share, got_ref, out_ref):
    count = got_ref.shape[0]
    height = out_ref.shape[1]
    for c in range(out_ref.shape[0]):
        for i in range(count):
            out_ref[c, i * main : (i + 1) * main, :] = got_ref[i, :main, :]
            at = count * main + i * sums
            out_ref[c, at : at + sums, :] = got_ref[i, main : main + sums, :]
            at = height - (count - i) * share
            out_ref[c, at : at + share, :] = got_ref[i, got_ref.shape[1] - share :, :]


def corpus_kernel(main, share, got_ref, corpus_ref, out_ref):
    cores, height, w = got_ref.shape
    rows = corpus_ref.shape[0]
    tile = min(main, 4 * w)
    reduced = jnp.zeros((rows, w), jnp.float32)
    for c in range(cores):
        for t in range(main // tile):
            row = main + t * tile // w
            mean = jnp.concatenate(
                [got_ref[c, row + q : row + q + 1, :] for q in range(tile // w)], axis=1
            )
            at = c * main + t * tile
            centered = split(corpus_ref[:, at : at + tile] - mean)
            image = split(got_ref[c, t * tile : (t + 1) * tile, :])
            reduced += dot_split(centered, image, ((1,), (0,)))
    for i in range(out_ref.shape[0]):
        for c in range(cores):
            out_ref[i, c * share : (c + 1) * share, :] = got_ref[c, height - share :, :]
        out_ref[i, cores * share :, :] = reduced


def solve_kernel(panel_ref, target_ref, stacked_ref, out_ref, work_ref, inverse_ref, own_ref):
    blocks, _, w = work_ref.shape
    kept = own_ref.shape[0]
    size = blocks * w
    half = w // 2
    for k in range(blocks):
        work_ref[k, k * w : (k + 1) * w, :] = stacked_ref[k, :w, :]
        work_ref[k, size:, :] = stacked_ref[k, 2 * w + half :, :]
        if k < 3:
            work_ref[k, (k + 1) * w : (k + 2) * w, :] = stacked_ref[k, w : 2 * w, :]
    work_ref[0, 3 * w : 4 * w, :] = stacked_ref[3, w : 2 * w, :]
    for k in range(2):
        for part in range(2):
            at = (k + 2) * w + part * half
            piece = stacked_ref[k + 2 * part, 2 * w : 2 * w + half, :]
            work_ref[k, at : at + half, :] = piece

    def finish(k):
        solved = dot_t(work_ref[k, (k + 1) * w :, :], inverse_ref[...])
        for m in range(k + 1, blocks):
            at = (m - k - 1) * w
            work_ref[m, m * w :, :] -= dot_t(solved[at:], solved[at : at + w])

        @pl.when(panel_ref[0] == k)
        def _():
            own_ref[...] = solved[-kept:]

    def step(k, carry):
        invert_factor(work_ref.at[k, pl.ds(pl.multiple_of(k * w, w), w)], inverse_ref)
        for q in range(blocks):
            pl.when(k == q)(functools.partial(finish, q))
        return carry

    lax.fori_loop(0, blocks, step, 0)
    slots = out_ref.shape[0]
    slot = lax.broadcasted_iota(jnp.int32, (slots, kept), 0)
    placing = (slot == target_ref[...]).astype(jnp.float32)
    out_ref[...] = jnp.dot(
        placing, own_ref[...], precision=HIGHEST, preferred_element_type=jnp.float32
    )


def call(kernel, shapes, *operands, scalars=0, scratch=(), flops=0):
    vmem = pl.BlockSpec(memory_space=pltpu.VMEM)
    smem = pl.BlockSpec(memory_space=pltpu.SMEM)
    outs = [jax.ShapeDtypeStruct(shape, jnp.float32) for shape in shapes]
    moved = 4 * sum(x.size for x in (*operands, *outs))
    got = pl.pallas_call(
        kernel,
        out_shape=outs,
        in_specs=[smem] * scalars + [vmem] * (len(operands) - scalars),
        out_specs=[vmem] * len(outs),
        scratch_shapes=[pltpu.VMEM(shape, jnp.float32) for shape in scratch],
        compiler_params=pltpu.CompilerParams(vmem_limit_bytes=40 << 20),
        cost_estimate=pl.CostEstimate(flops=flops, bytes_accessed=moved, transcendentals=0),
    )(*operands)
    return got if len(outs) > 1 else got[0]


def body(sample, start_basis, corpus, owner_shard):
    ny, nz, nc, panels = (lax.axis_size(name) for name in (*DP, "panel"))
    owners = ny * nz * nc
    slab, w = start_basis.shape
    depth = slab * owners
    rows = sample.shape[0]
    total_rows = rows * owners
    panel = lax.axis_index("panel").astype(jnp.int32).reshape(1)

    basis = spread(spread(spread(start_basis, "z"), "y"), "core")
    basis = basis.reshape(nc, ny * nz, slab, w)

    height = up8(depth // nc + depth // nc // w + 1)
    message = call(sample_kernel, [(nc, height, w)], sample, basis, flops=4 * rows * depth * w)
    main = depth // nc // ny
    message = call(halve_kernel, [(ny, up8(main + main // w + 1), w)], swap(message, "core"))
    message = call(
        functools.partial(slab_kernel, slab), [(nz, slab + 8, w)], swap(message, "y")
    )
    images, own = call(
        functools.partial(image_kernel, float(total_rows)),
        [(panels, slab, w), (slab + 8, w)],
        swap(message, "z"),
    )

    share = 5 * w // 2 // (nc * ny)
    gram = call(gram_kernel, [(5 * w // 2, w)], panel, swap(images, "panel"), scalars=1)
    gram = swap(gram.reshape(nc * ny, share, w), ("core", "y"))
    message = call(join_kernel, [(nz, slab + 8 + share, w)], gram, own)
    sums = main // w
    message = call(
        functools.partial(gather_z_kernel, slab),
        [(ny, main + up8(sums) + share, w)],
        swap(message, "z"),
    )
    message = call(
        functools.partial(gather_y_kernel, main, sums, share),
        [(nc, ny * (main + sums + share), w)],
        swap(message, "y"),
    )

    corpus_rows = corpus.shape[0]
    stacked = call(
        functools.partial(corpus_kernel, ny * main, ny * share),
        [(panels, 5 * w // 2 + corpus_rows, w)],
        swap(message, "core"),
        corpus,
        flops=2 * corpus_rows * depth * w,
    )
    stacked = swap(stacked, "panel")

    capacity = max(2, 2 * corpus_rows // owners)
    owner_ids = owner_shard[:, 0]
    choose = (owner_ids[:, None] == jnp.arange(owners, dtype=jnp.int32)[None, :]).astype(jnp.int32)
    running = jnp.cumsum(choose, axis=0)
    slot_index = jnp.sum(running * choose, axis=1) - 1
    target = (owner_ids * capacity + slot_index)[None, :]
    outgoing = call(
        solve_kernel,
        [(owners * capacity, w)],
        panel,
        target,
        stacked,
        scalars=1,
        scratch=[(panels, panels * w + corpus_rows, w), (w, w), (corpus_rows, w)],
        flops=panels * panels * w * w * (panels * w + corpus_rows),
    )
    arrived = swap(outgoing.reshape(owners, capacity, w), DP)
    return arrived.reshape(owners * capacity, w)


def solution(mesh):
    y, z, core, panel = 4, 16, 2, mesh.shape["panel"]
    fine = Mesh(mesh.devices.reshape(y, z, core, panel), (*DP, "panel"))
    placed = (P(DP, None), P(DP, "panel"), P(DP, None), P(DP, None))
    return jax.shard_map(
        body, mesh=fine, in_specs=placed, out_specs=P(DP, "panel"), check_vma=False
    )
```

time: 293 us -> 264 us (0.901)
  blocking collectives: 132 us -> 211 us
  waiting for transfers between devices: 80.1 us -> 16.6 us
  starting transfers between devices: 31.6 us -> 7.7 us
  local copies, waits for them, and re-layouts: 15.7 us -> 1.79 us
  other arithmetic: 7.36 us -> 0.39 us
  Pallas kernels: 20.2 us -> 25.9 us
  matrix products: 5.09 us -> 0 us
    all_to_all x6 -> x11, blocking collectives: 132 us -> 211 us  [swap(): return lax.all_to_all(parts, axis, 0, 0, tiled=True)]
    all_to_all x6 -> x2, waiting for transfers between devices: 80.1 us -> 16.6 us  [swap(): return lax.all_to_all(parts, axis, 0, 0, tiled=True)]
    all_to_all x6 -> x2, starting transfers between devices: 31.6 us -> 7.7 us  [swap(): return lax.all_to_all(parts, axis, 0, 0, tiled=True)]
    pallas_call x1 -> x10, Pallas kernels: 20.2 us -> 25.9 us  [call(): pl.pallas_call(kernel, out_shape=outs, in_specs=[smem] * scalars + [vmem]...]
    dot_general x5 -> x0, matrix products: 5.09 us -> none  [the longest x1 1.87 us: body(): projected = jnp.dot(sample, basis, precision=HIGH)]
    concatenate x5 -> x0, local copies, waits for them, and re-layouts: 4.36 us -> none  [pack(): return jnp.concatenate(pieces, axis=1)]
    reduce_sum x6 -> x0, other arithmetic: 4.36 us -> none  [the longest x1 2.4 us: body(): column_sums = jnp.sum(sample, axis=0)]
    broadcast_in_dim x7 -> x3, local copies, waits for them, and re-layouts: 5.2 us -> 1.11 us  [spread(): jnp.broadcast_to(block[None], (lax.axis_size(axis), *block.shape))]
  transfers between devices with their start and end apart: 6 -> 2, of which waited for: 6 -> 2; matrix products, arithmetic and copies ran while one was open for 1% -> 0% of each run, Pallas kernels for 0% -> 0%
where the time goes in v1:
time: 264 us; the launch traced here: 263 us
  blocking collectives  211 us (80%)
  Pallas kernels  25.9 us (10%)
  waiting for transfers between devices  16.6 us (6%)
  starting transfers between devices  7.7 us (3%)
    all_to_all x11, blocking collectives, swap(): return lax.all_to_all(parts, axis, 0, 0, tiled=True)  211 us
    pallas_call x10, Pallas kernels, call(): pl.pallas_call(kernel, out_shape=outs, in_specs=[smem] * scalars + [vmem]...  25.9 us
    all_to_all x2, waiting for transfers between devices, swap(): return lax.all_to_all(parts, axis, 0, 0, tiled=True)  16.6 us
    all_to_all x2, starting transfers between devices, swap(): return lax.all_to_all(parts, axis, 0, 0, tiled=True)  7.7 us
  transfers between devices with their start and end apart: 2, of which 2 were waited for; matrix products, arithmetic and copies ran while one was open for 0% of the time, Pallas kernels for 0%

profile of v1, /device:TPU:1, one launch (start us, length us, event | category | flops | bytes accessed | tf_op | source)
XLA Modules:
  0.0 263.2 jit_solution(13214626629427980159)
XLA Ops:
  0.0 0.7 broadcast_in_dim.6
  0.7 28.7 %all_to_all.65 = f32[16,32,128]{2,1,0:T(8,128)S(1)} all-to-all(f32[16,32,128]{2,1,0:T(8,128)S(1)} %broadcast_in_dim.6), channel_id=1, replica_groups=mesh['y'=4,'z'=16,'core'=2,'panel'=4] {'z'}, dimensions={0} | all-to-all | bytes 524288 | tf_op jit(solution)/shard_map/all_to_all | solution.py:16
  29.4 0.1 broadcast_in_dim.7
  29.5 13.7 %all_to_all.66 = f32[4,16,32,128]{3,2,1,0:T(8,128)S(1)} all-to-all(f32[4,16,32,128]{3,2,1,0:T(8,128)S(1)} %broadcast_in_dim.7), channel_id=1, replica_groups=mesh['y'=4,'z'=16,'core'=2,'panel'=4] {'y'}, dimensions={0} | all-to-all | bytes 2097152 | tf_op jit(solution)/shard_map/all_to_all | solution.py:16
  43.3 0.3 broadcast_in_dim.8
  43.5 0.0 copy-start
  43.6 12.9 %all_to_all.67 = f32[2,4,16,32,128]{4,3,2,1,0:T(8,128)S(1)} all-to-all(f32[2,4,16,32,128]{4,3,2,1,0:T(8,128)S(1)} %broadcast_in_dim.8), channel_id=1, replica_groups=mesh['y'=4,'z'=16,'core'=2,'panel'=4] {'core'}, dimensions={0} | all-to-all | bytes 4194304 | tf_op jit(solution)/shard_map/all_to_all | solution.py:16
  56.5 0.0 copy-done
  56.5 3.6 %shard_map.46 = f32[2,2072,128]{2,1,0:T(8,128)S(1)} custom-call(f32[256,4096]{1,0:T(8,128)S(1)} %copy-done, f32[2,64,32,128]{3,2,1,0:T(8,128)S(1)} %bitcast.10), custom_call_target="tpu_custom_call" | custom-call | flops 536870912 | bytes 8413184 | tf_op jit(solution)/shard_map/pallas_call | solution.py:289
  60.1 5.4 %all_to_all.68.got_ref = f32[2,2072,128]{2,1,0:T(8,128)S(1)} all-to-all(f32[2,2072,128]{2,1,0:T(8,128)S(1)} %shard_map.46), channel_id=1, replica_groups=mesh['y'=4,'z'=16,'core'=2,'panel'=4] {'core'}, dimensions={0} | all-to-all | bytes 4243456 | tf_op jit(solution)/shard_map/all_to_all | solution.py:16
  65.5 0.1 shard_map.47
  65.6 17.4 %all_to_all.69.got_ref = f32[4,520,128]{2,1,0:T(8,128)S(1)} all-to-all(f32[4,520,128]{2,1,0:T(8,128)S(1)} %shard_map.47), channel_id=1, replica_groups=mesh['y'=4,'z'=16,'core'=2,'panel'=4] {'y'}, dimensions={0} | all-to-all | bytes 2129920 | tf_op jit(solution)/shard_map/all_to_all | solution.py:16
  83.0 0.1 shard_map.48
  83.1 23.7 %all_to_all.70.got_ref = f32[16,40,128]{2,1,0:T(8,128)S(1)} all-to-all(f32[16,40,128]{2,1,0:T(8,128)S(1)} %shard_map.48), channel_id=1, replica_groups=mesh['y'=4,'z'=16,'core'=2,'panel'=4] {'z'}, dimensions={0} | all-to-all | bytes 655360 | tf_op jit(solution)/shard_map/all_to_all | solution.py:16
  106.8 0.7 shard_map.49
  107.5 4.0 %all-to-all-start.6 = ((f32[4,32,128]{2,1,0:T(8,128)}), f32[4,32,128]{2,1,0:T(8,128)S(1)}, u32[]{:S(2)}, u32[]{:S(2)}) async-start(f32[4,32,128]{2,1,0:T(8,128)} %get-tuple-element.7), calls=%async_computation.6 | async-start | bytes 131072 | tf_op jit(solution)/shard_map/all_to_all | solution.py:16
  111.6 4.5 %all-to-all-done.6.images_ref = f32[4,32,128]{2,1,0:T(8,128)S(1)} async-done(((f32[4,32,128]{2,1,0:T(8,128)}), f32[4,32,128]{2,1,0:T(8,128)S(1)}, u32[]{:S(2)}, u32[]{:S(2)}) %all-to-all-start.6) | async-done | bytes 65568 | tf_op jit(solution)/shard_map/all_to_all | solution.py:16
  116.0 0.4 shard_map.50
  116.4 16.9 %all_to_all.71.got_ref = f32[8,40,128]{2,1,0:T(8,128)S(1)} all-to-all(f32[8,40,128]{2,1,0:T(8,128)S(1)} %bitcast.11), channel_id=1, replica_groups=mesh['y'=4,'z'=16,'core'=2,'panel'=4] {'core','y'}, dimensions={0} | all-to-all | bytes 327680 | tf_op jit(solution)/shard_map/all_to_all | solution.py:16
  133.4 40.0 %all_to_all.72.got_ref = f32[16,80,128]{2,1,0:T(8,128)S(1)} all-to-all(f32[16,80,128]{2,1,0:T(8,128)S(1)} %shard_map.51), channel_id=1, replica_groups=mesh['y'=4,'z'=16,'core'=2,'panel'=4] {'z'}, dimensions={0} | all-to-all | bytes 1310720 | tf_op jit(solution)/shard_map/all_to_all | solution.py:16
  173.3 0.1 shard_map.52
  173.4 15.5 %all_to_all.73.got_ref = f32[4,560,128]{2,1,0:T(8,128)S(1)} all-to-all(f32[4,560,128]{2,1,0:T(8,128)S(1)} %shard_map.52), channel_id=1, replica_groups=mesh['y'=4,'z'=16,'core'=2,'panel'=4] {'y'}, dimensions={0} | all-to-all | bytes 2293760 | tf_op jit(solution)/shard_map/all_to_all | solution.py:16
  188.9 0.1 shard_map.53
  189.0 0.0 copy-start.1
  189.0 9.4 %all_to_all.74.got_ref = f32[2,2224,128]{2,1,0:T(8,128)S(1)} all-to-all(f32[2,2224,128]{2,1,0:T(8,128)S(1)} %shard_map.53), channel_id=1, replica_groups=mesh['y'=4,'z'=16,'core'=2,'panel'=4] {'core'}, dimensions={0} | all-to-all | bytes 4554752 | tf_op jit(solution)/shard_map/all_to_all | solution.py:16
  198.4 0.0 copy-done.1
  198.4 0.0 copy-start.2
  198.4 1.8 shard_map.54
  200.2 3.7 %all-to-all-start.11 = ((f32[4,416,128]{2,1,0:T(8,128)}), f32[4,416,128]{2,1,0:T(8,128)S(1)}, u32[]{:S(2)}, u32[]{:S(2)}) async-start(f32[4,416,128]{2,1,0:T(8,128)} %shard_map.54), calls=%async_computation.11 | async-start | bytes 1703936 | tf_op jit(solution)/shard_map/all_to_all | solution.py:16
  203.9 0.0 copy-done.2
  203.9 0.1 fusion
  204.0 0.1 reduce_window_sum.11
  204.1 0.2 select_reduce_fusion
  204.3 12.1 %all-to-all-done.11.stacked_ref = f32[4,416,128]{2,1,0:T(8,128)S(1)} async-done(((f32[4,416,128]{2,1,0:T(8,128)}), f32[4,416,128]{2,1,0:T(8,128)S(1)}, u32[]{:S(2)}, u32[]{:S(2)}) %all-to-all-start.11) | async-done | bytes 852000 | tf_op jit(solution)/shard_map/all_to_all | solution.py:16
  216.4 19.0 %shard_map.55 = f32[256,128]{1,0:T(8,128)S(1)} custom-call(s32[1]{0:T(128)} %bitcast.panel_ref, s32[1,96]{1,0:T(1,128)S(1)} %bitcast_add_fusion.target_ref, f32[4,416,128]{2,1,0:T(8,128)S(1)} %all-to-all-done.11.stacked_ref), custom_call_target="tpu_custom_call" | custom-call | flops 159383552 | bytes 983428 | tf_op jit(solution)/shard_map/pallas_call | solution.py:289
  235.4 27.1 %all_to_all.75 = f32[128,2,128]{2,1,0:T(2,128)S(1)} all-to-all(f32[128,2,128]{2,1,0:T(2,128)S(1)} %bitcast.12), channel_id=1, replica_groups=mesh['y'=4,'z'=16,'core'=2,'panel'=4] {'y','z','core'}, dimensions={0} | all-to-all | bytes 262144 | tf_op jit(solution)/shard_map/all_to_all | solution.py:16
  262.5 0.7 copy.6
  (2 shorter events, 0.0 us)
Async XLA Ops:
  43.5 12.9 %copy-start = (f32[256,4096]{1,0:T(8,128)S(1)}, f32[256,4096]{1,0:T(8,128)}, u32[]{:S(2)}) copy-start(f32[256,4096]{1,0:T(8,128)} %sample_ref.1) | copy-start | bytes 12582916
  107.5 8.5 %all-to-all-start.6 = ((f32[4,32,128]{2,1,0:T(8,128)}), f32[4,32,128]{2,1,0:T(8,128)S(1)}, u32[]{:S(2)}, u32[]{:S(2)}) async-start(f32[4,32,128]{2,1,0:T(8,128)} %get-tuple-element.7), calls=%async_computation.6 | async-start | bytes 131072 | tf_op jit(solution)/shard_map/all_to_all | solution.py:16
  189.0 9.4 %copy-start.1 = (f32[96,4096]{1,0:T(8,128)S(1)}, f32[96,4096]{1,0:T(8,128)}, u32[]{:S(2)}) copy-start(f32[96,4096]{1,0:T(8,128)} %corpus_ref.1) | copy-start | bytes 4718596
  198.4 5.5 %copy-start.2 = (s32[96,1]{0,1:T(1,128)S(1)}, s32[96,1]{0,1:T(1,128)}, u32[]{:S(2)}) copy-start(s32[96,1]{0,1:T(1,128)} %param.7) | copy-start | bytes 1156
  200.2 16.2 %all-to-all-start.11 = ((f32[4,416,128]{2,1,0:T(8,128)}), f32[4,416,128]{2,1,0:T(8,128)S(1)}, u32[]{:S(2)}, u32[]{:S(2)}) async-start(f32[4,416,128]{2,1,0:T(8,128)} %shard_map.54), calls=%async_computation.11 | async-start | bytes 1703936 | tf_op jit(solution)/shard_map/all_to_all | solution.py:16

commit v2 on v1

--- a/solution.py
+++ b/solution.py
@@ -168,57 +168,76 @@
     own_ref[slab:, :] = jnp.broadcast_to(mean, (own_ref.shape[0] - slab, w))
 
 
-def gram_kernel(panel_ref, images_ref, out_ref):
+def gram_kernel(panel_ref, images_ref, own_ref, out_ref):
     panel = panel_ref[0]
-    w = out_ref.shape[1]
+    count, height, w = out_ref.shape
+    half, slab = w // 2, images_ref.shape[1]
     own, after = images_ref[panel], images_ref[(panel + 1) % 4]
     last = panel == 3
     low = panel % 2
-    out_ref[:w, :] = tdot(own, own)
-    out_ref[w : 2 * w, :] = tdot(jnp.where(last, own, after), jnp.where(last, after, own))
+    square = tdot(own, own)
+    row = lax.broadcasted_iota(jnp.int32, (half, w), 0)
+    lane = lax.broadcasted_iota(jnp.int32, (half, w), 1)
+    folded = jnp.where((lane > row) | (lane >= half), square[:half], pltpu.roll(square[half:], half, 1))
+    diagonal = jnp.sum(jnp.where(unit(w), square, 0.0), axis=0, keepdims=True)
+    below = tdot(jnp.where(last, own, after), jnp.where(last, after, own))
     across = tdot(images_ref[low + 2], images_ref[low])
-    out_ref[2 * w :, :] = jnp.where(panel < 2, across[: w // 2], across[w // 2 :])
-
-
-def join_kernel(got_ref, own_ref, out_ref):
-    gram = sum(got_ref[i] for i in range(1, got_ref.shape[0])) + got_ref[0]
-    top = own_ref.shape[0]
-    for i in range(out_ref.shape[0]):
-        out_ref[i, :top, :] = own_ref[...]
-        out_ref[i, top:, :] = gram
-
-
-def gather_z_kernel(slab, got_ref, out_ref):
+    across = jnp.where(panel < 2, across[:half], across[half:])
+    gram = jnp.concatenate([folded, below, across], axis=0)
+    share = gram.shape[0] // count
+    for i in range(count):
+        out_ref[i, : slab + 1, :] = own_ref[: slab + 1, :]
+        out_ref[i, slab + 1 : slab + 8, :] = jnp.broadcast_to(diagonal, (7, w))
+        out_ref[i, slab + 8 :, :] = gram[i * share : (i + 1) * share]
+
+
+def unit(w):
+    row = lax.broadcasted_iota(jnp.int32, (w, w), 0)
+    return row == lax.broadcasted_iota(jnp.int32, (w, w), 1)
+
+
+def total(ref, at, rows):
+    return sum(ref[i, at : at + rows, :] for i in range(1, ref.shape[0])) + ref[0, at : at + rows, :]
+
+
+def gather_z_kernel(got_ref, out_ref):
     count, height, w = got_ref.shape
-    top = slab + 8
+    _, tall, _ = out_ref.shape
+    share = 2 * w // count
+    slab = height - 8 - share
     in_row = w // slab
-    gram = sum(got_ref[i, top:, :] for i in range(1, count)) + got_ref[0, top:, :]
-    main = count * slab
+    main, sums = count * slab, count // in_row
+    diagonal = total(got_ref, slab + 1, 1)
+    gram = total(got_ref, slab + 8, share)
     for c in range(out_ref.shape[0]):
         for i in range(count):
             out_ref[c, i * slab : (i + 1) * slab, :] = got_ref[i, :slab, :]
-        for r in range(count // in_row):
+        for r in range(sums):
             mean = sum(got_ref[r * in_row + q, slab : slab + 1, :] for q in range(in_row))
             out_ref[c, main + r : main + r + 1, :] = mean
-        at = out_ref.shape[1] - gram.shape[0]
-        for r in range(main + count // in_row, at):
-            out_ref[c, r : r + 1, :] = mean
-        out_ref[c, at:, :] = gram
+        fill = tall - share - main - sums
+        out_ref[c, main + sums : tall - share, :] = jnp.broadcast_to(diagonal, (fill, w))
+        out_ref[c, tall - share :, :] = gram
 
 
 def gather_y_kernel(main, sums, share, got_ref, out_ref):
-    count = got_ref.shape[0]
-    height = out_ref.shape[1]
+    count, height, w = got_ref.shape
+    tall = out_ref.shape[1]
+    diagonal = total(got_ref, main + sums, 1)
+    gram = total(got_ref, height - share, share)
     for c in range(out_ref.shape[0]):
         for i in range(count):
             out_ref[c, i * main : (i + 1) * main, :] = got_ref[i, :main, :]
             at = count * main + i * sums
             out_ref[c, at : at + sums, :] = got_ref[i, main : main + sums, :]
-            at = height - (count - i) * share
-            out_ref[c, at : at + share, :] = got_ref[i, got_ref.shape[1] - share :, :]
-
-
-def corpus_kernel(main, share, got_ref, corpus_ref, out_ref):
+        at = count * (main + sums)
+        out_ref[c, at : tall - share, :] = jnp.broadcast_to(diagonal, (tall - share - at, w))
+        out_ref[c, tall - share :, :] = gram
+
+
+def corpus_kernel(
+    main, sums, share, capacity, gram_rows, part_ref, target_ref, got_ref, corpus_ref, out_ref, diagonal_ref
+):
     cores, height, w = got_ref.shape
     rows = corpus_ref.shape[0]
     tile = min(main, 4 * w)
@@ -233,28 +252,64 @@
             centered = split(corpus_ref[:, at : at + tile] - mean)
             image = split(got_ref[c, t * tile : (t + 1) * tile, :])
             reduced += dot_split(centered, image, ((1,), (0,)))
-    for i in range(out_ref.shape[0]):
-        for c in range(cores):
-            out_ref[i, c * share : (c + 1) * share, :] = got_ref[c, height - share :, :]
-        out_ref[i, cores * share :, :] = reduced
-
-
-def solve_kernel(panel_ref, target_ref, stacked_ref, out_ref, work_ref, inverse_ref, own_ref):
+    diagonal_ref[...] = jnp.broadcast_to(total(got_ref, main + sums, 1), diagonal_ref.shape)
+    gram = total(got_ref, height - share, share)
+    tall = up8(gram_rows)
+    take = lax.broadcasted_iota(jnp.int32, (tall, share), 1) - part_ref[0] * gram_rows
+    take = (take == lax.broadcasted_iota(jnp.int32, (tall, share), 0)).astype(jnp.float32)
+    piece = jnp.dot(take, gram, precision=HIGHEST, preferred_element_type=jnp.float32)
+    source = jnp.concatenate([reduced, piece], axis=0)
+    shape = (out_ref.shape[0], rows + tall)
+    row = lax.broadcasted_iota(jnp.int32, shape, 0)
+    column = lax.broadcasted_iota(jnp.int32, shape, 1)
+    place = lax.rem(row, capacity + gram_rows) - capacity + rows
+    slots = (row == target_ref[...]).astype(jnp.float32)
+    shares = jnp.where(column < rows, 0.0, (place == column).astype(jnp.float32))
+    out_ref[...] = jnp.dot(
+        slots + shares, source, precision=HIGHEST, preferred_element_type=jnp.float32
+    )
+
+
+def arrange_kernel(capacity, gram_rows, counts, got_ref, diagonal_ref, out_ref):
+    wide = capacity + gram_rows
+    owners = got_ref.shape[0] // wide
+    top = owners * gram_rows
+    ny, nz, nc = counts
+    for c in range(out_ref.shape[0]):
+        for i in range(owners):
+            at = i * wide
+            y, z, core = i // (nz * nc), i // nc % nz, i % nc
+            row = ((z * ny + y) * nc + core) * gram_rows
+            out_ref[c, row : row + gram_rows, :] = got_ref[at + capacity : at + wide, :]
+            slot = top + i * capacity
+            out_ref[c, slot : slot + capacity, :] = got_ref[at : at + capacity, :]
+        out_ref[c, top + owners * capacity :, :] = diagonal_ref[...]
+
+
+def solve_kernel(panel_ref, stacked_ref, out_ref, work_ref, inverse_ref):
     blocks, _, w = work_ref.shape
-    kept = own_ref.shape[0]
+    kept = out_ref.shape[0]
     size = blocks * w
     half = w // 2
+    height = stacked_ref.shape[1]
+    row = lax.broadcasted_iota(jnp.int32, (half, w), 0)
+    lane = lax.broadcasted_iota(jnp.int32, (half, w), 1)
     for k in range(blocks):
-        work_ref[k, k * w : (k + 1) * w, :] = stacked_ref[k, :w, :]
-        work_ref[k, size:, :] = stacked_ref[k, 2 * w + half :, :]
+        folded = stacked_ref[k, :half, :]
+        upper = jnp.where((lane > row) | (lane >= half), folded, 0.0)
+        moved = pltpu.roll(folded, half, 1)
+        lower = jnp.where((lane >= half) & (lane - half < row), moved, 0.0)
+        square = jnp.concatenate([upper, lower], axis=0)
+        square = square + square.T + jnp.where(unit(w), stacked_ref[k, height - 1 :, :], 0.0)
+        work_ref[k, k * w : (k + 1) * w, :] = square
+        work_ref[k, size:, :] = stacked_ref[k, 2 * w : 2 * w + kept, :]
         if k < 3:
-            work_ref[k, (k + 1) * w : (k + 2) * w, :] = stacked_ref[k, w : 2 * w, :]
-    work_ref[0, 3 * w : 4 * w, :] = stacked_ref[3, w : 2 * w, :]
+            work_ref[k, (k + 1) * w : (k + 2) * w, :] = stacked_ref[k, half : half + w, :]
+    work_ref[0, 3 * w : 4 * w, :] = stacked_ref[3, half : half + w, :]
     for k in range(2):
         for part in range(2):
             at = (k + 2) * w + part * half
-            piece = stacked_ref[k + 2 * part, 2 * w : 2 * w + half, :]
-            work_ref[k, at : at + half, :] = piece
+            work_ref[k, at : at + half, :] = stacked_ref[k + 2 * part, half + w : 2 * w, :]
 
     def finish(k):
         solved = dot_t(work_ref[k, (k + 1) * w :, :], inverse_ref[...])
@@ -264,7 +319,7 @@
 
         @pl.when(panel_ref[0] == k)
         def _():
-            own_ref[...] = solved[-kept:]
+            out_ref[...] = solved[-kept:]
 
     def step(k, carry):
         invert_factor(work_ref.at[k, pl.ds(pl.multiple_of(k * w, w), w)], inverse_ref)
@@ -273,12 +328,6 @@
         return carry
 
     lax.fori_loop(0, blocks, step, 0)
-    slots = out_ref.shape[0]
-    slot = lax.broadcasted_iota(jnp.int32, (slots, kept), 0)
-    placing = (slot == target_ref[...]).astype(jnp.float32)
-    out_ref[...] = jnp.dot(
-        placing, own_ref[...], precision=HIGHEST, preferred_element_type=jnp.float32
-    )
 
 
 def call(kernel, shapes, *operands, scalars=0, scratch=(), flops=0):
@@ -323,50 +372,60 @@
         swap(message, "z"),
     )
 
-    share = 5 * w // 2 // (nc * ny)
-    gram = call(gram_kernel, [(5 * w // 2, w)], panel, swap(images, "panel"), scalars=1)
-    gram = swap(gram.reshape(nc * ny, share, w), ("core", "y"))
-    message = call(join_kernel, [(nz, slab + 8 + share, w)], gram, own)
+    share = 2 * w // nz
+    message = call(
+        gram_kernel,
+        [(nz, slab + 8 + share, w)],
+        panel,
+        swap(images, "panel"),
+        own,
+        scalars=1,
+    )
     sums = main // w
-    message = call(
-        functools.partial(gather_z_kernel, slab),
-        [(ny, main + up8(sums) + share, w)],
-        swap(message, "z"),
-    )
+    message = call(gather_z_kernel, [(ny, main + up8(sums + 1) + share, w)], swap(message, "z"))
     message = call(
         functools.partial(gather_y_kernel, main, sums, share),
-        [(nc, ny * (main + sums + share), w)],
+        [(nc, ny * main + up8(ny * sums + 1) + share, w)],
         swap(message, "y"),
     )
 
     corpus_rows = corpus.shape[0]
-    stacked = call(
-        functools.partial(corpus_kernel, ny * main, ny * share),
-        [(panels, 5 * w // 2 + corpus_rows, w)],
-        swap(message, "core"),
-        corpus,
-        flops=2 * corpus_rows * depth * w,
-    )
-    stacked = swap(stacked, "panel")
-
     capacity = max(2, 2 * corpus_rows // owners)
+    gram_rows = 2 * w // owners
+    wide = capacity + gram_rows
     owner_ids = owner_shard[:, 0]
     choose = (owner_ids[:, None] == jnp.arange(owners, dtype=jnp.int32)[None, :]).astype(jnp.int32)
     running = jnp.cumsum(choose, axis=0)
     slot_index = jnp.sum(running * choose, axis=1) - 1
-    target = (owner_ids * capacity + slot_index)[None, :]
-    outgoing = call(
+    target = jnp.pad(owner_ids * wide + slot_index, (0, up8(gram_rows)), constant_values=-1)[None, :]
+    part = lax.axis_index("y") * nc + lax.axis_index("core")
+    part = part.astype(jnp.int32).reshape(1)
+    outgoing, diagonal = call(
+        functools.partial(corpus_kernel, ny * main, ny * sums, share, capacity, gram_rows),
+        [(owners * wide, w), (8, w)],
+        part,
+        target,
+        swap(message, "core"),
+        corpus,
+        scalars=1,
+        flops=2 * corpus_rows * depth * w,
+    )
+    arrived = swap(outgoing.reshape(owners, wide, w), DP)
+    stacked = call(
+        functools.partial(arrange_kernel, capacity, gram_rows, (ny, nz, nc)),
+        [(panels, owners * wide + 8, w)],
+        arrived.reshape(owners * wide, w),
+        diagonal,
+    )
+    return call(
         solve_kernel,
         [(owners * capacity, w)],
         panel,
-        target,
-        stacked,
+        swap(stacked, "panel"),
         scalars=1,
-        scratch=[(panels, panels * w + corpus_rows, w), (w, w), (corpus_rows, w)],
-        flops=panels * panels * w * w * (panels * w + corpus_rows),
-    )
-    arrived = swap(outgoing.reshape(owners, capacity, w), DP)
-    return arrived.reshape(owners * capacity, w)
+        scratch=[(panels, panels * w + owners * capacity, w), (w, w)],
+        flops=panels * panels * w * w * (panels * w + owners * capacity),
+    )
 
 
 def solution(mesh):

time: 264 us -> 251 us (0.951)
  blocking collectives: 211 us -> 197 us
    all_to_all x11 -> x10, blocking collectives: 211 us -> 197 us  [swap(): return lax.all_to_all(parts, axis, 0, 0, tiled=True)]
where the time goes in v2:
time: 251 us; the launch traced here: 249 us
  blocking collectives  197 us (78%)
  Pallas kernels  28.1 us (11%)
  waiting for transfers between devices  14 us (6%)
  starting transfers between devices  7.54 us (3%)
    all_to_all x10, blocking collectives, swap(): return lax.all_to_all(parts, axis, 0, 0, tiled=True)  197 us
    pallas_call x10, Pallas kernels, call(): pl.pallas_call(kernel, out_shape=outs, in_specs=[smem] * scalars + [vmem]...  28.1 us
    all_to_all x2, waiting for transfers between devices, swap(): return lax.all_to_all(parts, axis, 0, 0, tiled=True)  14 us
    all_to_all x2, starting transfers between devices, swap(): return lax.all_to_all(parts, axis, 0, 0, tiled=True)  7.54 us
  transfers between devices with their start and end apart: 2, of which 2 were waited for; matrix products, arithmetic and copies ran while one was open for 0% of the time, Pallas kernels for 0%

profile of v2, /device:TPU:1, one launch (start us, length us, event | category | flops | bytes accessed | tf_op | source)
XLA Modules:
  0.0 248.7 jit_solution(8444181433913485638)
XLA Ops:
  0.0 0.7 broadcast_in_dim.9
  0.7 28.7 %all_to_all.60 = f32[16,32,128]{2,1,0:T(8,128)S(1)} all-to-all(f32[16,32,128]{2,1,0:T(8,128)S(1)} %broadcast_in_dim.9), channel_id=1, replica_groups=mesh['y'=4,'z'=16,'core'=2,'panel'=4] {'z'}, dimensions={0} | all-to-all | bytes 524288 | tf_op jit(solution)/shard_map/all_to_all | solution.py:16
  29.4 0.1 broadcast_in_dim.10
  29.5 13.7 %all_to_all.61 = f32[4,16,32,128]{3,2,1,0:T(8,128)S(1)} all-to-all(f32[4,16,32,128]{3,2,1,0:T(8,128)S(1)} %broadcast_in_dim.10), channel_id=1, replica_groups=mesh['y'=4,'z'=16,'core'=2,'panel'=4] {'y'}, dimensions={0} | all-to-all | bytes 2097152 | tf_op jit(solution)/shard_map/all_to_all | solution.py:16
  43.3 0.3 broadcast_in_dim.11
  43.5 0.0 copy-start
  43.6 12.9 %all_to_all.62 = f32[2,4,16,32,128]{4,3,2,1,0:T(8,128)S(1)} all-to-all(f32[2,4,16,32,128]{4,3,2,1,0:T(8,128)S(1)} %broadcast_in_dim.11), channel_id=1, replica_groups=mesh['y'=4,'z'=16,'core'=2,'panel'=4] {'core'}, dimensions={0} | all-to-all | bytes 4194304 | tf_op jit(solution)/shard_map/all_to_all | solution.py:16
  56.5 0.0 copy-done
  56.5 3.6 %shard_map.46 = f32[2,2072,128]{2,1,0:T(8,128)S(1)} custom-call(f32[256,4096]{1,0:T(8,128)S(1)} %copy-done, f32[2,64,32,128]{3,2,1,0:T(8,128)S(1)} %bitcast.9), custom_call_target="tpu_custom_call" | custom-call | flops 536870912 | bytes 8413184 | tf_op jit(solution)/shard_map/pallas_call | solution.py:338
  60.1 5.4 %all_to_all.63.got_ref = f32[2,2072,128]{2,1,0:T(8,128)S(1)} all-to-all(f32[2,2072,128]{2,1,0:T(8,128)S(1)} %shard_map.46), channel_id=1, replica_groups=mesh['y'=4,'z'=16,'core'=2,'panel'=4] {'core'}, dimensions={0} | all-to-all | bytes 4243456 | tf_op jit(solution)/shard_map/all_to_all | solution.py:16
  65.5 0.1 shard_map.47
  65.6 17.4 %all_to_all.64.got_ref = f32[4,520,128]{2,1,0:T(8,128)S(1)} all-to-all(f32[4,520,128]{2,1,0:T(8,128)S(1)} %shard_map.47), channel_id=1, replica_groups=mesh['y'=4,'z'=16,'core'=2,'panel'=4] {'y'}, dimensions={0} | all-to-all | bytes 2129920 | tf_op jit(solution)/shard_map/all_to_all | solution.py:16
  83.0 0.1 shard_map.48
  83.1 23.7 %all_to_all.65.got_ref = f32[16,40,128]{2,1,0:T(8,128)S(1)} all-to-all(f32[16,40,128]{2,1,0:T(8,128)S(1)} %shard_map.48), channel_id=1, replica_groups=mesh['y'=4,'z'=16,'core'=2,'panel'=4] {'z'}, dimensions={0} | all-to-all | bytes 655360 | tf_op jit(solution)/shard_map/all_to_all | solution.py:16
  106.8 0.7 shard_map.49
  107.5 4.0 %all-to-all-start.6 = ((f32[4,32,128]{2,1,0:T(8,128)}), f32[4,32,128]{2,1,0:T(8,128)S(1)}, u32[]{:S(2)}, u32[]{:S(2)}) async-start(f32[4,32,128]{2,1,0:T(8,128)} %get-tuple-element.9), calls=%async_computation.6 | async-start | bytes 131072 | tf_op jit(solution)/shard_map/all_to_all | solution.py:16
  111.6 4.5 %all-to-all-done.6.images_ref = f32[4,32,128]{2,1,0:T(8,128)S(1)} async-done(((f32[4,32,128]{2,1,0:T(8,128)}), f32[4,32,128]{2,1,0:T(8,128)S(1)}, u32[]{:S(2)}, u32[]{:S(2)}) %all-to-all-start.6) | async-done | bytes 65568 | tf_op jit(solution)/shard_map/all_to_all | solution.py:16
  116.0 0.4 shard_map.50
  116.4 32.0 %all_to_all.66.got_ref = f32[16,56,128]{2,1,0:T(8,128)S(1)} all-to-all(f32[16,56,128]{2,1,0:T(8,128)S(1)} %shard_map.50), channel_id=1, replica_groups=mesh['y'=4,'z'=16,'core'=2,'panel'=4] {'z'}, dimensions={0} | all-to-all | bytes 917504 | tf_op jit(solution)/shard_map/all_to_all | solution.py:16
  148.4 0.0 copy-start.2
  148.4 1.1 shard_map.51
  149.4 3.5 %all-to-all-start.8 = ((f32[4,536,128]{2,1,0:T(8,128)}), f32[4,536,128]{2,1,0:T(8,128)S(1)}, u32[]{:S(2)}, u32[]{:S(2)}) async-start(f32[4,536,128]{2,1,0:T(8,128)} %shard_map.51), calls=%async_computation.8 | async-start | bytes 2195456 | tf_op jit(solution)/shard_map/all_to_all | solution.py:16
  153.0 0.0 copy-done.2
  153.0 0.1 fusion
  153.1 0.1 reduce_window_sum.11
  153.2 0.2 select_reduce_fusion
  153.4 9.5 %all-to-all-done.8.got_ref = f32[4,536,128]{2,1,0:T(8,128)S(1)} async-done(((f32[4,536,128]{2,1,0:T(8,128)}), f32[4,536,128]{2,1,0:T(8,128)S(1)}, u32[]{:S(2)}, u32[]{:S(2)}) %all-to-all-start.8) | async-done | bytes 1097760 | tf_op jit(solution)/shard_map/all_to_all | solution.py:16
  162.9 0.1 shard_map.52
  163.1 0.0 copy-start.1
  163.1 13.4 %all_to_all.67.got_ref = f32[2,2088,128]{2,1,0:T(8,128)S(1)} all-to-all(f32[2,2088,128]{2,1,0:T(8,128)S(1)} %shard_map.52), channel_id=1, replica_groups=mesh['y'=4,'z'=16,'core'=2,'panel'=4] {'core'}, dimensions={0} | all-to-all | bytes 4276224 | tf_op jit(solution)/shard_map/all_to_all | solution.py:16
  176.5 0.0 copy-done.1
  176.5 1.4 shard_map.53
  177.9 35.0 %all_to_all.68 = f32[128,4,128]{2,1,0:T(4,128)S(1)} all-to-all(f32[128,4,128]{2,1,0:T(4,128)S(1)} %bitcast.11), channel_id=1, replica_groups=mesh['y'=4,'z'=16,'core'=2,'panel'=4] {'y','z','core'}, dimensions={0} | all-to-all | bytes 524288 | tf_op jit(solution)/shard_map/all_to_all | solution.py:16
  212.9 0.4 shard_map.54
  213.2 15.2 %all_to_all.69.stacked_ref = f32[4,520,128]{2,1,0:T(8,128)S(1)} all-to-all(f32[4,520,128]{2,1,0:T(8,128)S(1)} %shard_map.54), channel_id=1, replica_groups=mesh['y'=4,'z'=16,'core'=2,'panel'=4] {'panel'}, dimensions={0} | all-to-all | bytes 2129920 | tf_op jit(solution)/shard_map/all_to_all | solution.py:16
  228.5 20.3 %shard_map.55 = f32[256,128]{1,0:T(8,128)} custom-call(s32[1]{0:T(128)} %bitcast.panel_ref, f32[4,520,128]{2,1,0:T(8,128)S(1)} %all_to_all.69.stacked_ref), custom_call_target="tpu_custom_call" | custom-call | flops 201326592 | bytes 1196036 | tf_op jit(solution)/shard_map/pallas_call | solution.py:338
  (2 shorter events, 0.0 us)
Async XLA Ops:
  43.5 12.9 %copy-start = (f32[256,4096]{1,0:T(8,128)S(1)}, f32[256,4096]{1,0:T(8,128)}, u32[]{:S(2)}) copy-start(f32[256,4096]{1,0:T(8,128)} %sample_ref.1) | copy-start | bytes 12582916
  107.5 8.5 %all-to-all-start.6 = ((f32[4,32,128]{2,1,0:T(8,128)}), f32[4,32,128]{2,1,0:T(8,128)S(1)}, u32[]{:S(2)}, u32[]{:S(2)}) async-start(f32[4,32,128]{2,1,0:T(8,128)} %get-tuple-element.9), calls=%async_computation.6 | async-start | bytes 131072 | tf_op jit(solution)/shard_map/all_to_all | solution.py:16
  148.4 4.6 %copy-start.2 = (s32[96,1]{0,1:T(1,128)S(1)}, s32[96,1]{0,1:T(1,128)}, u32[]{:S(2)}) copy-start(s32[96,1]{0,1:T(1,128)} %param.7) | copy-start | bytes 1156
  149.4 13.5 %all-to-all-start.8 = ((f32[4,536,128]{2,1,0:T(8,128)}), f32[4,536,128]{2,1,0:T(8,128)S(1)}, u32[]{:S(2)}, u32[]{:S(2)}) async-start(f32[4,536,128]{2,1,0:T(8,128)} %shard_map.51), calls=%async_computation.8 | async-start | bytes 2195456 | tf_op jit(solution)/shard_map/all_to_all | solution.py:16
  163.1 13.4 %copy-start.1 = (f32[96,4096]{1,0:T(8,128)S(1)}, f32[96,4096]{1,0:T(8,128)}, u32[]{:S(2)}) copy-start(f32[96,4096]{1,0:T(8,128)} %corpus_ref.1) | copy-start | bytes 4718596

commit v3 on v2

--- a/solution.py
+++ b/solution.py
@@ -168,7 +168,7 @@
     own_ref[slab:, :] = jnp.broadcast_to(mean, (own_ref.shape[0] - slab, w))
 
 
-def gram_kernel(panel_ref, images_ref, own_ref, out_ref):
+def gram_kernel(pieces, panel_ref, images_ref, own_ref, out_ref, gram_ref):
     panel = panel_ref[0]
     count, height, w = out_ref.shape
     half, slab = w // 2, images_ref.shape[1]
@@ -183,12 +183,14 @@
     below = tdot(jnp.where(last, own, after), jnp.where(last, after, own))
     across = tdot(images_ref[low + 2], images_ref[low])
     across = jnp.where(panel < 2, across[:half], across[half:])
-    gram = jnp.concatenate([folded, below, across], axis=0)
-    share = gram.shape[0] // count
+    gram_ref[...] = jnp.concatenate([folded, below, across], axis=0)
+    each = gram_ref.shape[0] // count // pieces
     for i in range(count):
         out_ref[i, : slab + 1, :] = own_ref[: slab + 1, :]
         out_ref[i, slab + 1 : slab + 8, :] = jnp.broadcast_to(diagonal, (7, w))
-        out_ref[i, slab + 8 :, :] = gram[i * share : (i + 1) * share]
+        for q in range(pieces):
+            at, row = slab + 8 + q * each, (q * count + i) * each
+            out_ref[i, at : at + each, :] = gram_ref[row : row + each, :]
 
 
 def unit(w):
@@ -236,7 +238,7 @@
 
 
 def corpus_kernel(
-    main, sums, share, capacity, gram_rows, part_ref, target_ref, got_ref, corpus_ref, out_ref, diagonal_ref
+    main, sums, share, lead, height_out, gram_rows, part_ref, target_ref, got_ref, corpus_ref, out_ref, diagonal_ref
 ):
     cores, height, w = got_ref.shape
     rows = corpus_ref.shape[0]
@@ -262,7 +264,7 @@
     shape = (out_ref.shape[0], rows + tall)
     row = lax.broadcasted_iota(jnp.int32, shape, 0)
     column = lax.broadcasted_iota(jnp.int32, shape, 1)
-    place = lax.rem(row, capacity + gram_rows) - capacity + rows
+    place = lax.rem(row, height_out) - lead + rows
     slots = (row == target_ref[...]).astype(jnp.float32)
     shares = jnp.where(column < rows, 0.0, (place == column).astype(jnp.float32))
     out_ref[...] = jnp.dot(
@@ -270,39 +272,54 @@
     )
 
 
-def arrange_kernel(capacity, gram_rows, counts, got_ref, diagonal_ref, out_ref):
-    wide = capacity + gram_rows
-    owners = got_ref.shape[0] // wide
-    top = owners * gram_rows
-    ny, nz, nc = counts
-    for c in range(out_ref.shape[0]):
-        for i in range(owners):
-            at = i * wide
-            y, z, core = i // (nz * nc), i // nc % nz, i % nc
-            row = ((z * ny + y) * nc + core) * gram_rows
-            out_ref[c, row : row + gram_rows, :] = got_ref[at + capacity : at + wide, :]
-            slot = top + i * capacity
-            out_ref[c, slot : slot + capacity, :] = got_ref[at : at + capacity, :]
-        out_ref[c, top + owners * capacity :, :] = diagonal_ref[...]
-
-
-def solve_kernel(panel_ref, stacked_ref, out_ref, work_ref, inverse_ref):
+def arrange_kernel(capacity, gram_rows, got_ref, diagonal_ref, out_ref):
+    count = got_ref.shape[0]
+    peers = out_ref.shape[0]
+    panels = 4
+    lead = peers // panels * capacity
+    top = count * capacity
+    full = top + count * gram_rows
+    for i in range(count):
+        for q in range(peers // panels):
+            rows = got_ref[i, q * capacity : (q + 1) * capacity, :]
+            out_ref[q * panels, i * capacity : (i + 1) * capacity, :] = rows
+        rows = got_ref[i, lead : lead + gram_rows, :]
+        out_ref[0, top + i * gram_rows : top + (i + 1) * gram_rows, :] = rows
+    for q in range(peers):
+        first = q // panels * panels
+        if q != first:
+            out_ref[q, :top, :] = out_ref[first, :top, :]
+        if q:
+            out_ref[q, top:full, :] = out_ref[0, top:full, :]
+        out_ref[q, full:, :] = diagonal_ref[...]
+
+
+def solve_kernel(
+    counts, panel_ref, got_ref, out_ref, work_ref, inverse_ref, stacked_ref, own_ref
+):
     blocks, _, w = work_ref.shape
     kept = out_ref.shape[0]
     size = blocks * w
     half = w // 2
-    height = stacked_ref.shape[1]
+    ny, nz, nc = counts
+    top = kept // (ny * nc)
+    share = 2 * w // (ny * nc)
     row = lax.broadcasted_iota(jnp.int32, (half, w), 0)
     lane = lax.broadcasted_iota(jnp.int32, (half, w), 1)
     for k in range(blocks):
+        for q in range(ny * nc):
+            source = q * blocks + k
+            stacked_ref[k, q * share : (q + 1) * share, :] = got_ref[source, top : top + share, :]
+            at = size + q * top
+            work_ref[k, at : at + top, :] = got_ref[source, :top, :]
         folded = stacked_ref[k, :half, :]
         upper = jnp.where((lane > row) | (lane >= half), folded, 0.0)
         moved = pltpu.roll(folded, half, 1)
         lower = jnp.where((lane >= half) & (lane - half < row), moved, 0.0)
         square = jnp.concatenate([upper, lower], axis=0)
-        square = square + square.T + jnp.where(unit(w), stacked_ref[k, height - 1 :, :], 0.0)
+        diagonal = got_ref[k, top + share : top + share + 1, :]
+        square = square + square.T + jnp.where(unit(w), diagonal, 0.0)
         work_ref[k, k * w : (k + 1) * w, :] = square
-        work_ref[k, size:, :] = stacked_ref[k, 2 * w : 2 * w + kept, :]
         if k < 3:
             work_ref[k, (k + 1) * w : (k + 2) * w, :] = stacked_ref[k, half : half + w, :]
     work_ref[0, 3 * w : 4 * w, :] = stacked_ref[3, half : half + w, :]
@@ -319,7 +336,7 @@
 
         @pl.when(panel_ref[0] == k)
         def _():
-            out_ref[...] = solved[-kept:]
+            own_ref[...] = solved[-kept:]
 
     def step(k, carry):
         invert_factor(work_ref.at[k, pl.ds(pl.multiple_of(k * w, w), w)], inverse_ref)
@@ -328,6 +345,11 @@
         return carry
 
     lax.fori_loop(0, blocks, step, 0)
+    slots = kept // (ny * nz * nc)
+    for i in range(ny * nz * nc):
+        y, z, core = i // (nz * nc), i // nc % nz, i % nc
+        at = ((y * nc + core) * nz + z) * slots
+        out_ref[i * slots : (i + 1) * slots, :] = own_ref[at : at + slots, :]
 
 
 def call(kernel, shapes, *operands, scalars=0, scratch=(), flops=0):
@@ -374,12 +396,13 @@
 
     share = 2 * w // nz
     message = call(
-        gram_kernel,
+        functools.partial(gram_kernel, ny * nc),
         [(nz, slab + 8 + share, w)],
         panel,
         swap(images, "panel"),
         own,
         scalars=1,
+        scratch=[(2 * w, w)],
     )
     sums = main // w
     message = call(gather_z_kernel, [(ny, main + up8(sums + 1) + share, w)], swap(message, "z"))
@@ -392,17 +415,20 @@
     corpus_rows = corpus.shape[0]
     capacity = max(2, 2 * corpus_rows // owners)
     gram_rows = 2 * w // owners
-    wide = capacity + gram_rows
+    lead = ny * nc * capacity
+    height = up8(lead + gram_rows)
     owner_ids = owner_shard[:, 0]
     choose = (owner_ids[:, None] == jnp.arange(owners, dtype=jnp.int32)[None, :]).astype(jnp.int32)
     running = jnp.cumsum(choose, axis=0)
     slot_index = jnp.sum(running * choose, axis=1) - 1
-    target = jnp.pad(owner_ids * wide + slot_index, (0, up8(gram_rows)), constant_values=-1)[None, :]
+    plane = owner_ids // (nz * nc) * nc + owner_ids % nc
+    target = owner_ids // nc % nz * height + plane * capacity + slot_index
+    target = jnp.pad(target, (0, up8(gram_rows)), constant_values=-1)[None, :]
     part = lax.axis_index("y") * nc + lax.axis_index("core")
     part = part.astype(jnp.int32).reshape(1)
     outgoing, diagonal = call(
-        functools.partial(corpus_kernel, ny * main, ny * sums, share, capacity, gram_rows),
-        [(owners * wide, w), (8, w)],
+        functools.partial(corpus_kernel, ny * main, ny * sums, share, lead, height, gram_rows),
+        [(nz * height, w), (8, w)],
         part,
         target,
         swap(message, "core"),
@@ -410,21 +436,21 @@
         scalars=1,
         flops=2 * corpus_rows * depth * w,
     )
-    arrived = swap(outgoing.reshape(owners, wide, w), DP)
-    stacked = call(
-        functools.partial(arrange_kernel, capacity, gram_rows, (ny, nz, nc)),
-        [(panels, owners * wide + 8, w)],
-        arrived.reshape(owners * wide, w),
+    message = call(
+        functools.partial(arrange_kernel, capacity, gram_rows),
+        [(ny * nc * panels, nz * (capacity + gram_rows) + 8, w)],
+        swap(outgoing.reshape(nz, height, w), "z"),
         diagonal,
     )
+    slots = owners * capacity
     return call(
-        solve_kernel,
-        [(owners * capacity, w)],
+        functools.partial(solve_kernel, (ny, nz, nc)),
+        [(slots, w)],
         panel,
-        swap(stacked, "panel"),
+        swap(message, ("y", "core", "panel")),
         scalars=1,
-        scratch=[(panels, panels * w + owners * capacity, w), (w, w)],
-        flops=panels * panels * w * w * (panels * w + owners * capacity),
+        scratch=[(panels, panels * w + slots, w), (w, w), (panels, 2 * w, w), (slots, w)],
+        flops=panels * panels * w * w * (panels * w + slots),
     )
 
 

time: 251 us -> 247 us (0.984)
  no operation moved by 1% of the time
where the time goes in v3:
time: 247 us
  blocking collectives  196 us (79%)
  Pallas kernels  27.9 us (11%)
  waiting for transfers between devices  14 us (6%)
  starting transfers between devices  7.54 us (3%)
    all_to_all x10, blocking collectives, swap(): return lax.all_to_all(parts, axis, 0, 0, tiled=True)  196 us
    pallas_call x10, Pallas kernels, call(): pl.pallas_call(kernel, out_shape=outs, in_specs=[smem] * scalars + [vmem]...  27.9 us
    all_to_all x2, waiting for transfers between devices, swap(): return lax.all_to_all(parts, axis, 0, 0, tiled=True)  14 us
    all_to_all x2, starting transfers between devices, swap(): return lax.all_to_all(parts, axis, 0, 0, tiled=True)  7.54 us
  transfers between devices with their start and end apart: 2, of which 2 were waited for; matrix products, arithmetic and copies ran while one was open for 0% of the time, Pallas kernels for 0%

profile of v3, /device:TPU:1, one launch (start us, length us, event | category | flops | bytes accessed | tf_op | source)
XLA Modules:
  0.0 246.6 jit_solution(6503886260583265881)
XLA Ops:
  0.0 0.7 broadcast_in_dim.9
  0.7 28.7 %all_to_all.60 = f32[16,32,128]{2,1,0:T(8,128)S(1)} all-to-all(f32[16,32,128]{2,1,0:T(8,128)S(1)} %broadcast_in_dim.9), channel_id=1, replica_groups=mesh['y'=4,'z'=16,'core'=2,'panel'=4] {'z'}, dimensions={0} | all-to-all | bytes 524288 | tf_op jit(solution)/shard_map/all_to_all | solution.py:16
  29.4 0.1 broadcast_in_dim.10
  29.5 13.7 %all_to_all.61 = f32[4,16,32,128]{3,2,1,0:T(8,128)S(1)} all-to-all(f32[4,16,32,128]{3,2,1,0:T(8,128)S(1)} %broadcast_in_dim.10), channel_id=1, replica_groups=mesh['y'=4,'z'=16,'core'=2,'panel'=4] {'y'}, dimensions={0} | all-to-all | bytes 2097152 | tf_op jit(solution)/shard_map/all_to_all | solution.py:16
  43.3 0.3 broadcast_in_dim.11
  43.5 0.0 copy-start
  43.6 12.9 %all_to_all.62 = f32[2,4,16,32,128]{4,3,2,1,0:T(8,128)S(1)} all-to-all(f32[2,4,16,32,128]{4,3,2,1,0:T(8,128)S(1)} %broadcast_in_dim.11), channel_id=1, replica_groups=mesh['y'=4,'z'=16,'core'=2,'panel'=4] {'core'}, dimensions={0} | all-to-all | bytes 4194304 | tf_op jit(solution)/shard_map/all_to_all | solution.py:16
  56.5 0.0 copy-done
  56.5 3.6 %shard_map.46 = f32[2,2072,128]{2,1,0:T(8,128)S(1)} custom-call(f32[256,4096]{1,0:T(8,128)S(1)} %copy-done, f32[2,64,32,128]{3,2,1,0:T(8,128)S(1)} %bitcast.8), custom_call_target="tpu_custom_call" | custom-call | flops 536870912 | bytes 8413184 | tf_op jit(solution)/shard_map/pallas_call | solution.py:360
  60.1 5.4 %all_to_all.63.got_ref = f32[2,2072,128]{2,1,0:T(8,128)S(1)} all-to-all(f32[2,2072,128]{2,1,0:T(8,128)S(1)} %shard_map.46), channel_id=1, replica_groups=mesh['y'=4,'z'=16,'core'=2,'panel'=4] {'core'}, dimensions={0} | all-to-all | bytes 4243456 | tf_op jit(solution)/shard_map/all_to_all | solution.py:16
  65.5 0.1 shard_map.47
  65.6 17.4 %all_to_all.64.got_ref = f32[4,520,128]{2,1,0:T(8,128)S(1)} all-to-all(f32[4,520,128]{2,1,0:T(8,128)S(1)} %shard_map.47), channel_id=1, replica_groups=mesh['y'=4,'z'=16,'core'=2,'panel'=4] {'y'}, dimensions={0} | all-to-all | bytes 2129920 | tf_op jit(solution)/shard_map/all_to_all | solution.py:16
  83.0 0.1 shard_map.48
  83.1 23.7 %all_to_all.65.got_ref = f32[16,40,128]{2,1,0:T(8,128)S(1)} all-to-all(f32[16,40,128]{2,1,0:T(8,128)S(1)} %shard_map.48), channel_id=1, replica_groups=mesh['y'=4,'z'=16,'core'=2,'panel'=4] {'z'}, dimensions={0} | all-to-all | bytes 655360 | tf_op jit(solution)/shard_map/all_to_all | solution.py:16
  106.8 0.7 shard_map.49
  107.5 4.0 %all-to-all-start.6 = ((f32[4,32,128]{2,1,0:T(8,128)}), f32[4,32,128]{2,1,0:T(8,128)S(1)}, u32[]{:S(2)}, u32[]{:S(2)}) async-start(f32[4,32,128]{2,1,0:T(8,128)} %get-tuple-element.9), calls=%async_computation.6 | async-start | bytes 131072 | tf_op jit(solution)/shard_map/all_to_all | solution.py:16
  111.6 4.5 %all-to-all-done.6.images_ref = f32[4,32,128]{2,1,0:T(8,128)S(1)} async-done(((f32[4,32,128]{2,1,0:T(8,128)}), f32[4,32,128]{2,1,0:T(8,128)S(1)}, u32[]{:S(2)}, u32[]{:S(2)}) %all-to-all-start.6) | async-done | bytes 65568 | tf_op jit(solution)/shard_map/all_to_all | solution.py:16
  116.0 0.4 shard_map.50
  116.4 32.0 %all_to_all.66.got_ref = f32[16,56,128]{2,1,0:T(8,128)S(1)} all-to-all(f32[16,56,128]{2,1,0:T(8,128)S(1)} %shard_map.50), channel_id=1, replica_groups=mesh['y'=4,'z'=16,'core'=2,'panel'=4] {'z'}, dimensions={0} | all-to-all | bytes 917504 | tf_op jit(solution)/shard_map/all_to_all | solution.py:16
  148.4 0.0 copy-start.2
  148.4 1.1 shard_map.51
  149.5 3.5 %all-to-all-start.8 = ((f32[4,536,128]{2,1,0:T(8,128)}), f32[4,536,128]{2,1,0:T(8,128)S(1)}, u32[]{:S(2)}, u32[]{:S(2)}) async-start(f32[4,536,128]{2,1,0:T(8,128)} %shard_map.51), calls=%async_computation.8 | async-start | bytes 2195456 | tf_op jit(solution)/shard_map/all_to_all | solution.py:16
  153.0 0.0 copy-done.2
  153.0 0.1 fusion
  153.1 0.1 reduce_window_sum.11
  153.2 0.2 select_reduce_fusion
  153.4 9.5 %all-to-all-done.8.got_ref = f32[4,536,128]{2,1,0:T(8,128)S(1)} async-done(((f32[4,536,128]{2,1,0:T(8,128)}), f32[4,536,128]{2,1,0:T(8,128)S(1)}, u32[]{:S(2)}, u32[]{:S(2)}) %all-to-all-start.8) | async-done | bytes 1097760 | tf_op jit(solution)/shard_map/all_to_all | solution.py:16
  163.0 0.1 shard_map.52
  163.1 0.0 copy-start.1
  163.1 13.4 %all_to_all.67.got_ref = f32[2,2088,128]{2,1,0:T(8,128)S(1)} all-to-all(f32[2,2088,128]{2,1,0:T(8,128)S(1)} %shard_map.52), channel_id=1, replica_groups=mesh['y'=4,'z'=16,'core'=2,'panel'=4] {'core'}, dimensions={0} | all-to-all | bytes 4276224 | tf_op jit(solution)/shard_map/all_to_all | solution.py:16
  176.5 0.0 copy-done.1
  176.5 1.4 shard_map.53
  177.9 22.9 %all_to_all.68.got_ref = f32[16,24,128]{2,1,0:T(8,128)S(1)} all-to-all(f32[16,24,128]{2,1,0:T(8,128)S(1)} %bitcast.9), channel_id=1, replica_groups=mesh['y'=4,'z'=16,'core'=2,'panel'=4] {'z'}, dimensions={0} | all-to-all | bytes 393216 | tf_op jit(solution)/shard_map/all_to_all | solution.py:16
  200.8 0.1 shard_map.54
  200.9 25.4 %all_to_all.69.got_ref = f32[32,72,128]{2,1,0:T(8,128)S(1)} all-to-all(f32[32,72,128]{2,1,0:T(8,128)S(1)} %shard_map.54), channel_id=1, replica_groups=mesh['y'=4,'z'=16,'core'=2,'panel'=4] {'y','core','panel'}, dimensions={0} | all-to-all | bytes 2359296 | tf_op jit(solution)/shard_map/all_to_all | solution.py:16
  226.3 20.3 %shard_map.55 = f32[256,128]{1,0:T(8,128)} custom-call(s32[1]{0:T(128)} %bitcast.panel_ref, f32[32,72,128]{2,1,0:T(8,128)S(1)} %all_to_all.69.got_ref), custom_call_target="tpu_custom_call" | custom-call | flops 201326592 | bytes 1310724 | tf_op jit(solution)/shard_map/pallas_call | solution.py:360
  (2 shorter events, 0.0 us)
Async XLA Ops:
  43.5 12.9 %copy-start = (f32[256,4096]{1,0:T(8,128)S(1)}, f32[256,4096]{1,0:T(8,128)}, u32[]{:S(2)}) copy-start(f32[256,4096]{1,0:T(8,128)} %sample_ref.1) | copy-start | bytes 12582916
  107.5 8.5 %all-to-all-start.6 = ((f32[4,32,128]{2,1,0:T(8,128)}), f32[4,32,128]{2,1,0:T(8,128)S(1)}, u32[]{:S(2)}, u32[]{:S(2)}) async-start(f32[4,32,128]{2,1,0:T(8,128)} %get-tuple-element.9), calls=%async_computation.6 | async-start | bytes 131072 | tf_op jit(solution)/shard_map/all_to_all | solution.py:16
  148.4 4.6 %copy-start.2 = (s32[96,1]{0,1:T(1,128)S(1)}, s32[96,1]{0,1:T(1,128)}, u32[]{:S(2)}) copy-start(s32[96,1]{0,1:T(1,128)} %param.7) | copy-start | bytes 1156
  149.5 13.5 %all-to-all-start.8 = ((f32[4,536,128]{2,1,0:T(8,128)}), f32[4,536,128]{2,1,0:T(8,128)S(1)}, u32[]{:S(2)}, u32[]{:S(2)}) async-start(f32[4,536,128]{2,1,0:T(8,128)} %shard_map.51), calls=%async_computation.8 | async-start | bytes 2195456 | tf_op jit(solution)/shard_map/all_to_all | solution.py:16
  163.1 13.4 %copy-start.1 = (f32[96,4096]{1,0:T(8,128)S(1)}, f32[96,4096]{1,0:T(8,128)}, u32[]{:S(2)}) copy-start(f32[96,4096]{1,0:T(8,128)} %corpus_ref.1) | copy-start | bytes 4718596

commit v4 on v3

--- a/solution.py
+++ b/solution.py
@@ -141,31 +141,30 @@
     count, _, w = out_ref.shape
     got = sum(got_ref[i] for i in range(1, got_ref.shape[0])) + got_ref[0]
     main = slab * count
-    in_row = w // slab
-    lifted = got[main + main // w : main + main // w + 1]
-    lane = lax.broadcasted_iota(jnp.int32, (1, w), 1) // slab
+    sums = main // w
+    lifted = got[main + sums : main + sums + 1]
     for i in range(count):
-        row = main + i // in_row
-        sums = jnp.where(lane == i % in_row, got[row : row + 1], 0.0)
         out_ref[i, :slab, :] = got[i * slab : (i + 1) * slab]
-        out_ref[i, slab : slab + 1, :] = sums
-        out_ref[i, slab + 1 :, :] = jnp.broadcast_to(lifted, (out_ref.shape[1] - slab - 1, w))
-
-
-def image_kernel(total_rows, got_ref, spread_ref, own_ref):
+        out_ref[i, slab : slab + sums, :] = got[main : main + sums]
+        out_ref[i, slab + sums :, :] = jnp.broadcast_to(lifted, (8 - sums, w))
+
+
+def image_kernel(total_rows, sums, place_ref, got_ref, spread_ref, own_ref, mean_ref):
     copies, slab, w = spread_ref.shape
     got = sum(got_ref[i] for i in range(1, got_ref.shape[0])) + got_ref[0]
-    mean = got[slab : slab + 1] / total_rows
-    lifted = got[slab + 1 : slab + 2] / total_rows
-    here = lax.broadcasted_iota(jnp.int32, (slab, w), 1) % slab == lax.broadcasted_iota(
-        jnp.int32, (slab, w), 0
-    )
-    column = jnp.sum(jnp.where(here, mean, 0.0), axis=1, keepdims=True)
+    mean = got[slab : slab + 8] / total_rows
+    lifted = got[slab + sums : slab + sums + 1] / total_rows
+    in_row = w // slab
+    at = lax.broadcasted_iota(jnp.int32, (8, w), 0)
+    mine = jnp.sum(jnp.where(at == place_ref[0] // in_row, mean, 0.0), axis=0, keepdims=True)
+    lane = lax.broadcasted_iota(jnp.int32, (slab, w), 1) - place_ref[0] % in_row * slab
+    here = lane == lax.broadcasted_iota(jnp.int32, (slab, w), 0)
+    column = jnp.sum(jnp.where(here, mine, 0.0), axis=1, keepdims=True)
     image = got[:slab] / total_rows - column * lifted
     for i in range(copies):
         spread_ref[i] = image
-    own_ref[:slab, :] = image
-    own_ref[slab:, :] = jnp.broadcast_to(mean, (own_ref.shape[0] - slab, w))
+    own_ref[...] = image
+    mean_ref[...] = mean
 
 
 def gram_kernel(pieces, panel_ref, images_ref, own_ref, out_ref, gram_ref):
@@ -179,17 +178,15 @@
     row = lax.broadcasted_iota(jnp.int32, (half, w), 0)
     lane = lax.broadcasted_iota(jnp.int32, (half, w), 1)
     folded = jnp.where((lane > row) | (lane >= half), square[:half], pltpu.roll(square[half:], half, 1))
-    diagonal = jnp.sum(jnp.where(unit(w), square, 0.0), axis=0, keepdims=True)
     below = tdot(jnp.where(last, own, after), jnp.where(last, after, own))
     across = tdot(images_ref[low + 2], images_ref[low])
     across = jnp.where(panel < 2, across[:half], across[half:])
     gram_ref[...] = jnp.concatenate([folded, below, across], axis=0)
     each = gram_ref.shape[0] // count // pieces
     for i in range(count):
-        out_ref[i, : slab + 1, :] = own_ref[: slab + 1, :]
-        out_ref[i, slab + 1 : slab + 8, :] = jnp.broadcast_to(diagonal, (7, w))
+        out_ref[i, :slab, :] = own_ref[...]
         for q in range(pieces):
-            at, row = slab + 8 + q * each, (q * count + i) * each
+            at, row = slab + q * each, (q * count + i) * each
             out_ref[i, at : at + each, :] = gram_ref[row : row + each, :]
 
 
@@ -202,48 +199,39 @@
     return sum(ref[i, at : at + rows, :] for i in range(1, ref.shape[0])) + ref[0, at : at + rows, :]
 
 
-def gather_z_kernel(got_ref, out_ref):
+def gather_z_kernel(got_ref, mean_ref, out_ref):
     count, height, w = got_ref.shape
-    _, tall, _ = out_ref.shape
     share = 2 * w // count
-    slab = height - 8 - share
-    in_row = w // slab
-    main, sums = count * slab, count // in_row
-    diagonal = total(got_ref, slab + 1, 1)
-    gram = total(got_ref, slab + 8, share)
+    slab = height - share
+    main = count * slab
+    gram = total(got_ref, slab, share)
     for c in range(out_ref.shape[0]):
         for i in range(count):
             out_ref[c, i * slab : (i + 1) * slab, :] = got_ref[i, :slab, :]
-        for r in range(sums):
-            mean = sum(got_ref[r * in_row + q, slab : slab + 1, :] for q in range(in_row))
-            out_ref[c, main + r : main + r + 1, :] = mean
-        fill = tall - share - main - sums
-        out_ref[c, main + sums : tall - share, :] = jnp.broadcast_to(diagonal, (fill, w))
-        out_ref[c, tall - share :, :] = gram
+        out_ref[c, main : main + 8, :] = mean_ref[...]
+        out_ref[c, main + 8 :, :] = gram
 
 
 def gather_y_kernel(main, sums, share, got_ref, out_ref):
     count, height, w = got_ref.shape
     tall = out_ref.shape[1]
-    diagonal = total(got_ref, main + sums, 1)
     gram = total(got_ref, height - share, share)
     for c in range(out_ref.shape[0]):
         for i in range(count):
             out_ref[c, i * main : (i + 1) * main, :] = got_ref[i, :main, :]
             at = count * main + i * sums
             out_ref[c, at : at + sums, :] = got_ref[i, main : main + sums, :]
-        at = count * (main + sums)
-        out_ref[c, at : tall - share, :] = jnp.broadcast_to(diagonal, (tall - share - at, w))
         out_ref[c, tall - share :, :] = gram
 
 
 def corpus_kernel(
-    main, sums, share, lead, height_out, gram_rows, part_ref, target_ref, got_ref, corpus_ref, out_ref, diagonal_ref
+    main, share, lead, height_out, gram_rows, part_ref, target_ref, got_ref, corpus_ref, out_ref, diagonal_ref
 ):
     cores, height, w = got_ref.shape
     rows = corpus_ref.shape[0]
     tile = min(main, 4 * w)
     reduced = jnp.zeros((rows, w), jnp.float32)
+    diagonal = jnp.zeros((1, w), jnp.float32)
     for c in range(cores):
         for t in range(main // tile):
             row = main + t * tile // w
@@ -252,9 +240,10 @@
             )
             at = c * main + t * tile
             centered = split(corpus_ref[:, at : at + tile] - mean)
-            image = split(got_ref[c, t * tile : (t + 1) * tile, :])
-            reduced += dot_split(centered, image, ((1,), (0,)))
-    diagonal_ref[...] = jnp.broadcast_to(total(got_ref, main + sums, 1), diagonal_ref.shape)
+            image = got_ref[c, t * tile : (t + 1) * tile, :]
+            diagonal += jnp.sum(image * image, axis=0, keepdims=True)
+            reduced += dot_split(centered, split(image), ((1,), (0,)))
+    diagonal_ref[...] = jnp.broadcast_to(diagonal, diagonal_ref.shape)
     gram = total(got_ref, height - share, share)
     tall = up8(gram_rows)
     take = lax.broadcasted_iota(jnp.int32, (tall, share), 1) - part_ref[0] * gram_rows
@@ -388,27 +377,29 @@
     message = call(
         functools.partial(slab_kernel, slab), [(nz, slab + 8, w)], swap(message, "y")
     )
-    images, own = call(
-        functools.partial(image_kernel, float(total_rows)),
-        [(panels, slab, w), (slab + 8, w)],
+    sums = main // w
+    images, own, mean = call(
+        functools.partial(image_kernel, float(total_rows), sums),
+        [(panels, slab, w), (slab, w), (8, w)],
+        lax.axis_index("z").astype(jnp.int32).reshape(1),
         swap(message, "z"),
+        scalars=1,
     )
 
     share = 2 * w // nz
     message = call(
         functools.partial(gram_kernel, ny * nc),
-        [(nz, slab + 8 + share, w)],
+        [(nz, slab + share, w)],
         panel,
         swap(images, "panel"),
         own,
         scalars=1,
         scratch=[(2 * w, w)],
     )
-    sums = main // w
-    message = call(gather_z_kernel, [(ny, main + up8(sums + 1) + share, w)], swap(message, "z"))
+    message = call(gather_z_kernel, [(ny, main + 8 + share, w)], swap(message, "z"), mean)
     message = call(
         functools.partial(gather_y_kernel, main, sums, share),
-        [(nc, ny * main + up8(ny * sums + 1) + share, w)],
+        [(nc, ny * main + up8(ny * sums) + share, w)],
         swap(message, "y"),
     )
 
@@ -427,7 +418,7 @@
     part = lax.axis_index("y") * nc + lax.axis_index("core")
     part = part.astype(jnp.int32).reshape(1)
     outgoing, diagonal = call(
-        functools.partial(corpus_kernel, ny * main, ny * sums, share, lead, height, gram_rows),
+        functools.partial(corpus_kernel, ny * main, share, lead, height, gram_rows),
         [(nz * height, w), (8, w)],
         part,
         target,

time: 247 us -> 246 us (level)
  blocking collectives: 196 us -> 169 us
  waiting for transfers between devices: 14 us -> 28.3 us
  starting transfers between devices: 7.54 us -> 17.2 us
    all_to_all x10 -> x9, blocking collectives: 196 us -> 169 us  [swap(): return lax.all_to_all(parts, axis, 0, 0, tiled=True)]
    all_to_all x2 -> x3, waiting for transfers between devices: 14 us -> 28.3 us  [swap(): return lax.all_to_all(parts, axis, 0, 0, tiled=True)]
    all_to_all x2 -> x3, starting transfers between devices: 7.54 us -> 17.2 us  [swap(): return lax.all_to_all(parts, axis, 0, 0, tiled=True)]
  transfers between devices with their start and end apart: 2 -> 3, of which waited for: 2 -> 3; matrix products, arithmetic and copies ran while one was open for 0% -> 0% of each run, Pallas kernels for 0% -> 0%
where the time goes in v4:
time: 246 us; the launch traced here: 245 us
  blocking collectives  169 us (69%)
  Pallas kernels  28.8 us (12%)
  waiting for transfers between devices  28.3 us (12%)
  starting transfers between devices  17.2 us (7%)
    all_to_all x9, blocking collectives, swap(): return lax.all_to_all(parts, axis, 0, 0, tiled=True)  169 us
    pallas_call x10, Pallas kernels, call(): pl.pallas_call(kernel, out_shape=outs, in_specs=[smem] * scalars + [vmem]...  28.8 us
    all_to_all x3, waiting for transfers between devices, swap(): return lax.all_to_all(parts, axis, 0, 0, tiled=True)  28.3 us
    all_to_all x3, starting transfers between devices, swap(): return lax.all_to_all(parts, axis, 0, 0, tiled=True)  17.2 us
  transfers between devices with their start and end apart: 3, of which 3 were waited for; matrix products, arithmetic and copies ran while one was open for 0% of the time, Pallas kernels for 0%

profile of v4, /device:TPU:1, one launch (start us, length us, event | category | flops | bytes accessed | tf_op | source)
XLA Modules:
  0.0 245.1 jit_solution(9666926046526693621)
XLA Ops:
  0.0 0.7 broadcast_in_dim.9
  0.7 28.7 %all_to_all.60 = f32[16,32,128]{2,1,0:T(8,128)S(1)} all-to-all(f32[16,32,128]{2,1,0:T(8,128)S(1)} %broadcast_in_dim.9), channel_id=1, replica_groups=mesh['y'=4,'z'=16,'core'=2,'panel'=4] {'z'}, dimensions={0} | all-to-all | bytes 524288 | tf_op jit(solution)/shard_map/all_to_all | solution.py:16
  29.4 0.1 broadcast_in_dim.10
  29.5 13.7 %all_to_all.61 = f32[4,16,32,128]{3,2,1,0:T(8,128)S(1)} all-to-all(f32[4,16,32,128]{3,2,1,0:T(8,128)S(1)} %broadcast_in_dim.10), channel_id=1, replica_groups=mesh['y'=4,'z'=16,'core'=2,'panel'=4] {'y'}, dimensions={0} | all-to-all | bytes 2097152 | tf_op jit(solution)/shard_map/all_to_all | solution.py:16
  43.3 0.3 broadcast_in_dim.11
  43.5 0.0 copy-start
  43.6 12.9 %all_to_all.62 = f32[2,4,16,32,128]{4,3,2,1,0:T(8,128)S(1)} all-to-all(f32[2,4,16,32,128]{4,3,2,1,0:T(8,128)S(1)} %broadcast_in_dim.11), channel_id=1, replica_groups=mesh['y'=4,'z'=16,'core'=2,'panel'=4] {'core'}, dimensions={0} | all-to-all | bytes 4194304 | tf_op jit(solution)/shard_map/all_to_all | solution.py:16
  56.5 0.0 copy-done
  56.5 3.6 %shard_map.46 = f32[2,2072,128]{2,1,0:T(8,128)S(1)} custom-call(f32[256,4096]{1,0:T(8,128)S(1)} %copy-done, f32[2,64,32,128]{3,2,1,0:T(8,128)S(1)} %bitcast.9), custom_call_target="tpu_custom_call" | custom-call | flops 536870912 | bytes 8413184 | tf_op jit(solution)/shard_map/pallas_call | solution.py:349
  60.1 5.4 %all_to_all.63.got_ref = f32[2,2072,128]{2,1,0:T(8,128)S(1)} all-to-all(f32[2,2072,128]{2,1,0:T(8,128)S(1)} %shard_map.46), channel_id=1, replica_groups=mesh['y'=4,'z'=16,'core'=2,'panel'=4] {'core'}, dimensions={0} | all-to-all | bytes 4243456 | tf_op jit(solution)/shard_map/all_to_all | solution.py:16
  65.5 0.1 shard_map.47
  65.6 17.4 %all_to_all.64.got_ref = f32[4,520,128]{2,1,0:T(8,128)S(1)} all-to-all(f32[4,520,128]{2,1,0:T(8,128)S(1)} %shard_map.47), channel_id=1, replica_groups=mesh['y'=4,'z'=16,'core'=2,'panel'=4] {'y'}, dimensions={0} | all-to-all | bytes 2129920 | tf_op jit(solution)/shard_map/all_to_all | solution.py:16
  83.0 0.8 shard_map.48
  83.8 9.6 %all-to-all-start.5 = ((f32[16,40,128]{2,1,0:T(8,128)}), f32[16,40,128]{2,1,0:T(8,128)S(1)}, u32[]{:S(2)}, u32[]{:S(2)}) async-start(f32[16,40,128]{2,1,0:T(8,128)} %shard_map.48), calls=%async_computation.5 | async-start | bytes 655360 | tf_op jit(solution)/shard_map/all_to_all | solution.py:16
  93.5 14.3 %all-to-all-done.5.got_ref = f32[16,40,128]{2,1,0:T(8,128)S(1)} async-done(((f32[16,40,128]{2,1,0:T(8,128)}), f32[16,40,128]{2,1,0:T(8,128)S(1)}, u32[]{:S(2)}, u32[]{:S(2)}) %all-to-all-start.5) | async-done | bytes 327712 | tf_op jit(solution)/shard_map/all_to_all | solution.py:16
  107.7 0.7 shard_map.49
  108.5 4.0 %all-to-all-start.6 = ((f32[4,32,128]{2,1,0:T(8,128)}), f32[4,32,128]{2,1,0:T(8,128)S(1)}, u32[]{:S(2)}, u32[]{:S(2)}) async-start(f32[4,32,128]{2,1,0:T(8,128)} %get-tuple-element.10), calls=%async_computation.6 | async-start | bytes 131072 | tf_op jit(solution)/shard_map/all_to_all | solution.py:16
  112.5 4.5 %all-to-all-done.6.images_ref = f32[4,32,128]{2,1,0:T(8,128)S(1)} async-done(((f32[4,32,128]{2,1,0:T(8,128)}), f32[4,32,128]{2,1,0:T(8,128)S(1)}, u32[]{:S(2)}, u32[]{:S(2)}) %all-to-all-start.6) | async-done | bytes 65568 | tf_op jit(solution)/shard_map/all_to_all | solution.py:16
  117.0 0.4 shard_map.50
  117.4 0.0 copy-start.2
  117.4 29.9 %all_to_all.65.got_ref = f32[16,48,128]{2,1,0:T(8,128)S(1)} all-to-all(f32[16,48,128]{2,1,0:T(8,128)S(1)} %shard_map.50), channel_id=1, replica_groups=mesh['y'=4,'z'=16,'core'=2,'panel'=4] {'z'}, dimensions={0} | all-to-all | bytes 786432 | tf_op jit(solution)/shard_map/all_to_all | solution.py:16
  147.2 1.1 shard_map.51
  148.3 3.5 %all-to-all-start.8 = ((f32[4,536,128]{2,1,0:T(8,128)}), f32[4,536,128]{2,1,0:T(8,128)S(1)}, u32[]{:S(2)}, u32[]{:S(2)}) async-start(f32[4,536,128]{2,1,0:T(8,128)} %shard_map.51), calls=%async_computation.8 | async-start | bytes 2195456 | tf_op jit(solution)/shard_map/all_to_all | solution.py:16
  151.8 0.0 copy-done.2
  151.8 0.1 fusion
  151.9 0.1 reduce_window_sum.11
  152.1 0.2 select_reduce_fusion
  152.3 9.5 %all-to-all-done.8.got_ref = f32[4,536,128]{2,1,0:T(8,128)S(1)} async-done(((f32[4,536,128]{2,1,0:T(8,128)}), f32[4,536,128]{2,1,0:T(8,128)S(1)}, u32[]{:S(2)}, u32[]{:S(2)}) %all-to-all-start.8) | async-done | bytes 1097760 | tf_op jit(solution)/shard_map/all_to_all | solution.py:16
  161.8 0.1 shard_map.52
  161.9 0.0 copy-start.1
  162.0 13.5 %all_to_all.66.got_ref = f32[2,2080,128]{2,1,0:T(8,128)S(1)} all-to-all(f32[2,2080,128]{2,1,0:T(8,128)S(1)} %shard_map.52), channel_id=1, replica_groups=mesh['y'=4,'z'=16,'core'=2,'panel'=4] {'core'}, dimensions={0} | all-to-all | bytes 4259840 | tf_op jit(solution)/shard_map/all_to_all | solution.py:16
  175.5 0.0 copy-done.1
  175.5 1.5 shard_map.53
  177.0 22.3 %all_to_all.67.got_ref = f32[16,24,128]{2,1,0:T(8,128)S(1)} all-to-all(f32[16,24,128]{2,1,0:T(8,128)S(1)} %bitcast.10), channel_id=1, replica_groups=mesh['y'=4,'z'=16,'core'=2,'panel'=4] {'z'}, dimensions={0} | all-to-all | bytes 393216 | tf_op jit(solution)/shard_map/all_to_all | solution.py:16
  199.3 0.1 shard_map.54
  199.4 25.3 %all_to_all.68.got_ref = f32[32,72,128]{2,1,0:T(8,128)S(1)} all-to-all(f32[32,72,128]{2,1,0:T(8,128)S(1)} %shard_map.54), channel_id=1, replica_groups=mesh['y'=4,'z'=16,'core'=2,'panel'=4] {'y','core','panel'}, dimensions={0} | all-to-all | bytes 2359296 | tf_op jit(solution)/shard_map/all_to_all | solution.py:16
  224.7 20.3 %shard_map.55 = f32[256,128]{1,0:T(8,128)} custom-call(s32[1]{0:T(128)} %bitcast.panel_ref, f32[32,72,128]{2,1,0:T(8,128)S(1)} %all_to_all.68.got_ref), custom_call_target="tpu_custom_call" | custom-call | flops 201326592 | bytes 1310724 | tf_op jit(solution)/shard_map/pallas_call | solution.py:349
  (2 shorter events, 0.0 us)
Async XLA Ops:
  43.5 12.9 %copy-start = (f32[256,4096]{1,0:T(8,128)S(1)}, f32[256,4096]{1,0:T(8,128)}, u32[]{:S(2)}) copy-start(f32[256,4096]{1,0:T(8,128)} %sample_ref.1) | copy-start | bytes 12582916
  83.8 23.9 %all-to-all-start.5 = ((f32[16,40,128]{2,1,0:T(8,128)}), f32[16,40,128]{2,1,0:T(8,128)S(1)}, u32[]{:S(2)}, u32[]{:S(2)}) async-start(f32[16,40,128]{2,1,0:T(8,128)} %shard_map.48), calls=%async_computation.5 | async-start | bytes 655360 | tf_op jit(solution)/shard_map/all_to_all | solution.py:16
  108.5 8.5 %all-to-all-start.6 = ((f32[4,32,128]{2,1,0:T(8,128)}), f32[4,32,128]{2,1,0:T(8,128)S(1)}, u32[]{:S(2)}, u32[]{:S(2)}) async-start(f32[4,32,128]{2,1,0:T(8,128)} %get-tuple-element.10), calls=%async_computation.6 | async-start | bytes 131072 | tf_op jit(solution)/shard_map/all_to_all | solution.py:16
  117.4 34.5 %copy-start.2 = (s32[96,1]{0,1:T(1,128)S(1)}, s32[96,1]{0,1:T(1,128)}, u32[]{:S(2)}) copy-start(s32[96,1]{0,1:T(1,128)} %param.7) | copy-start | bytes 1156
  148.3 13.5 %all-to-all-start.8 = ((f32[4,536,128]{2,1,0:T(8,128)}), f32[4,536,128]{2,1,0:T(8,128)S(1)}, u32[]{:S(2)}, u32[]{:S(2)}) async-start(f32[4,536,128]{2,1,0:T(8,128)} %shard_map.51), calls=%async_computation.8 | async-start | bytes 2195456 | tf_op jit(solution)/shard_map/all_to_all | solution.py:16
  161.9 13.5 %copy-start.1 = (f32[96,4096]{1,0:T(8,128)S(1)}, f32[96,4096]{1,0:T(8,128)}, u32[]{:S(2)}) copy-start(f32[96,4096]{1,0:T(8,128)} %corpus_ref.1) | copy-start | bytes 4718596

commit v5 on v4

--- a/solution.py
+++ b/solution.py
@@ -49,7 +49,9 @@
         ]
         scale = []
         for i in range(8):
-            scale.append(1.0 / pivot[i][i])
+            if i % 2 == 0:
+                p, q, r = pivot[i][i], pivot[i + 1][i], pivot[i + 1][i + 1]
+                scale += [1.0 / p, p * (1.0 / (p * r - q * q))]
             for j in range(i + 1, 8):
                 factor = pivot[j][i] * scale[i]
                 for k in range(i + 1, j + 1):
@@ -316,6 +318,13 @@
         for part in range(2):
             at = (k + 2) * w + part * half
             work_ref[k, at : at + half, :] = stacked_ref[k + 2 * part, half + w : 2 * w, :]
+    roots = [lax.rsqrt(got_ref[k, top + share : top + share + 1, :]) for k in range(blocks)]
+    turned = [jnp.sum(jnp.where(unit(w), x, 0.0), axis=1, keepdims=True) for x in roots]
+    for k in range(blocks):
+        for m in range(k, blocks):
+            block = work_ref[k, m * w : (m + 1) * w, :]
+            work_ref[k, m * w : (m + 1) * w, :] = block * roots[k] * turned[m]
+        work_ref[k, size:, :] = work_ref[k, size:, :] * roots[k]
 
     def finish(k):
         solved = dot_t(work_ref[k, (k + 1) * w :, :], inverse_ref[...])

time: 246 us -> 245 us (level)
  no operation moved by 1% of the time
where the time goes in v5:
time: 245 us; the launch traced here: 244 us
  blocking collectives  169 us (69%)
  waiting for transfers between devices  28.3 us (12%)
  Pallas kernels  27.6 us (11%)
  starting transfers between devices  17.2 us (7%)
    all_to_all x9, blocking collectives, swap(): return lax.all_to_all(parts, axis, 0, 0, tiled=True)  169 us
    all_to_all x3, waiting for transfers between devices, swap(): return lax.all_to_all(parts, axis, 0, 0, tiled=True)  28.3 us
    pallas_call x10, Pallas kernels, call(): pl.pallas_call(kernel, out_shape=outs, in_specs=[smem] * scalars + [vmem]...  27.6 us
    all_to_all x3, starting transfers between devices, swap(): return lax.all_to_all(parts, axis, 0, 0, tiled=True)  17.2 us
  transfers between devices with their start and end apart: 3, of which 3 were waited for; matrix products, arithmetic and copies ran while one was open for 0% of the time, Pallas kernels for 0%

profile of v5, /device:TPU:1, one launch (start us, length us, event | category | flops | bytes accessed | tf_op | source)
XLA Modules:
  0.0 243.8 jit_solution(15659019174298709206)
XLA Ops:
  0.0 0.7 broadcast_in_dim.9
  0.7 28.7 %all_to_all.60 = f32[16,32,128]{2,1,0:T(8,128)S(1)} all-to-all(f32[16,32,128]{2,1,0:T(8,128)S(1)} %broadcast_in_dim.9), channel_id=1, replica_groups=mesh['y'=4,'z'=16,'core'=2,'panel'=4] {'z'}, dimensions={0} | all-to-all | bytes 524288 | tf_op jit(solution)/shard_map/all_to_all | solution.py:16
  29.4 0.1 broadcast_in_dim.10
  29.5 13.7 %all_to_all.61 = f32[4,16,32,128]{3,2,1,0:T(8,128)S(1)} all-to-all(f32[4,16,32,128]{3,2,1,0:T(8,128)S(1)} %broadcast_in_dim.10), channel_id=1, replica_groups=mesh['y'=4,'z'=16,'core'=2,'panel'=4] {'y'}, dimensions={0} | all-to-all | bytes 2097152 | tf_op jit(solution)/shard_map/all_to_all | solution.py:16
  43.3 0.3 broadcast_in_dim.11
  43.5 0.0 copy-start
  43.6 12.9 %all_to_all.62 = f32[2,4,16,32,128]{4,3,2,1,0:T(8,128)S(1)} all-to-all(f32[2,4,16,32,128]{4,3,2,1,0:T(8,128)S(1)} %broadcast_in_dim.11), channel_id=1, replica_groups=mesh['y'=4,'z'=16,'core'=2,'panel'=4] {'core'}, dimensions={0} | all-to-all | bytes 4194304 | tf_op jit(solution)/shard_map/all_to_all | solution.py:16
  56.5 0.0 copy-done
  56.5 3.6 %shard_map.46 = f32[2,2072,128]{2,1,0:T(8,128)S(1)} custom-call(f32[256,4096]{1,0:T(8,128)S(1)} %copy-done, f32[2,64,32,128]{3,2,1,0:T(8,128)S(1)} %bitcast.9), custom_call_target="tpu_custom_call" | custom-call | flops 536870912 | bytes 8413184 | tf_op jit(solution)/shard_map/pallas_call | solution.py:358
  60.1 5.4 %all_to_all.63.got_ref = f32[2,2072,128]{2,1,0:T(8,128)S(1)} all-to-all(f32[2,2072,128]{2,1,0:T(8,128)S(1)} %shard_map.46), channel_id=1, replica_groups=mesh['y'=4,'z'=16,'core'=2,'panel'=4] {'core'}, dimensions={0} | all-to-all | bytes 4243456 | tf_op jit(solution)/shard_map/all_to_all | solution.py:16
  65.5 0.1 shard_map.47
  65.6 17.4 %all_to_all.64.got_ref = f32[4,520,128]{2,1,0:T(8,128)S(1)} all-to-all(f32[4,520,128]{2,1,0:T(8,128)S(1)} %shard_map.47), channel_id=1, replica_groups=mesh['y'=4,'z'=16,'core'=2,'panel'=4] {'y'}, dimensions={0} | all-to-all | bytes 2129920 | tf_op jit(solution)/shard_map/all_to_all | solution.py:16
  83.0 0.8 shard_map.48
  83.8 9.6 %all-to-all-start.5 = ((f32[16,40,128]{2,1,0:T(8,128)}), f32[16,40,128]{2,1,0:T(8,128)S(1)}, u32[]{:S(2)}, u32[]{:S(2)}) async-start(f32[16,40,128]{2,1,0:T(8,128)} %shard_map.48), calls=%async_computation.5 | async-start | bytes 655360 | tf_op jit(solution)/shard_map/all_to_all | solution.py:16
  93.5 14.3 %all-to-all-done.5.got_ref = f32[16,40,128]{2,1,0:T(8,128)S(1)} async-done(((f32[16,40,128]{2,1,0:T(8,128)}), f32[16,40,128]{2,1,0:T(8,128)S(1)}, u32[]{:S(2)}, u32[]{:S(2)}) %all-to-all-start.5) | async-done | bytes 327712 | tf_op jit(solution)/shard_map/all_to_all | solution.py:16
  107.7 0.7 shard_map.49
  108.5 4.0 %all-to-all-start.6 = ((f32[4,32,128]{2,1,0:T(8,128)}), f32[4,32,128]{2,1,0:T(8,128)S(1)}, u32[]{:S(2)}, u32[]{:S(2)}) async-start(f32[4,32,128]{2,1,0:T(8,128)} %get-tuple-element.10), calls=%async_computation.6 | async-start | bytes 131072 | tf_op jit(solution)/shard_map/all_to_all | solution.py:16
  112.5 4.5 %all-to-all-done.6.images_ref = f32[4,32,128]{2,1,0:T(8,128)S(1)} async-done(((f32[4,32,128]{2,1,0:T(8,128)}), f32[4,32,128]{2,1,0:T(8,128)S(1)}, u32[]{:S(2)}, u32[]{:S(2)}) %all-to-all-start.6) | async-done | bytes 65568 | tf_op jit(solution)/shard_map/all_to_all | solution.py:16
  117.0 0.4 shard_map.50
  117.4 0.0 copy-start.2
  117.4 29.9 %all_to_all.65.got_ref = f32[16,48,128]{2,1,0:T(8,128)S(1)} all-to-all(f32[16,48,128]{2,1,0:T(8,128)S(1)} %shard_map.50), channel_id=1, replica_groups=mesh['y'=4,'z'=16,'core'=2,'panel'=4] {'z'}, dimensions={0} | all-to-all | bytes 786432 | tf_op jit(solution)/shard_map/all_to_all | solution.py:16
  147.2 1.1 shard_map.51
  148.3 3.5 %all-to-all-start.8 = ((f32[4,536,128]{2,1,0:T(8,128)}), f32[4,536,128]{2,1,0:T(8,128)S(1)}, u32[]{:S(2)}, u32[]{:S(2)}) async-start(f32[4,536,128]{2,1,0:T(8,128)} %shard_map.51), calls=%async_computation.8 | async-start | bytes 2195456 | tf_op jit(solution)/shard_map/all_to_all | solution.py:16
  151.8 0.0 copy-done.2
  151.8 0.1 fusion
  151.9 0.1 reduce_window_sum.11
  152.1 0.2 select_reduce_fusion
  152.3 9.5 %all-to-all-done.8.got_ref = f32[4,536,128]{2,1,0:T(8,128)S(1)} async-done(((f32[4,536,128]{2,1,0:T(8,128)}), f32[4,536,128]{2,1,0:T(8,128)S(1)}, u32[]{:S(2)}, u32[]{:S(2)}) %all-to-all-start.8) | async-done | bytes 1097760 | tf_op jit(solution)/shard_map/all_to_all | solution.py:16
  161.8 0.1 shard_map.52
  161.9 0.0 copy-start.1
  162.0 13.5 %all_to_all.66.got_ref = f32[2,2080,128]{2,1,0:T(8,128)S(1)} all-to-all(f32[2,2080,128]{2,1,0:T(8,128)S(1)} %shard_map.52), channel_id=1, replica_groups=mesh['y'=4,'z'=16,'core'=2,'panel'=4] {'core'}, dimensions={0} | all-to-all | bytes 4259840 | tf_op jit(solution)/shard_map/all_to_all | solution.py:16
  175.5 0.0 copy-done.1
  175.5 1.5 shard_map.53
  177.0 22.3 %all_to_all.67.got_ref = f32[16,24,128]{2,1,0:T(8,128)S(1)} all-to-all(f32[16,24,128]{2,1,0:T(8,128)S(1)} %bitcast.10), channel_id=1, replica_groups=mesh['y'=4,'z'=16,'core'=2,'panel'=4] {'z'}, dimensions={0} | all-to-all | bytes 393216 | tf_op jit(solution)/shard_map/all_to_all | solution.py:16
  199.3 0.1 shard_map.54
  199.4 25.3 %all_to_all.68.got_ref = f32[32,72,128]{2,1,0:T(8,128)S(1)} all-to-all(f32[32,72,128]{2,1,0:T(8,128)S(1)} %shard_map.54), channel_id=1, replica_groups=mesh['y'=4,'z'=16,'core'=2,'panel'=4] {'y','core','panel'}, dimensions={0} | all-to-all | bytes 2359296 | tf_op jit(solution)/shard_map/all_to_all | solution.py:16
  224.7 19.1 %shard_map.55 = f32[256,128]{1,0:T(8,128)} custom-call(s32[1]{0:T(128)} %bitcast.panel_ref, f32[32,72,128]{2,1,0:T(8,128)S(1)} %all_to_all.68.got_ref), custom_call_target="tpu_custom_call" | custom-call | flops 201326592 | bytes 1310724 | tf_op jit(solution)/shard_map/pallas_call | solution.py:358
  (2 shorter events, 0.0 us)
Async XLA Ops:
  43.5 12.9 %copy-start = (f32[256,4096]{1,0:T(8,128)S(1)}, f32[256,4096]{1,0:T(8,128)}, u32[]{:S(2)}) copy-start(f32[256,4096]{1,0:T(8,128)} %sample_ref.1) | copy-start | bytes 12582916
  83.8 23.9 %all-to-all-start.5 = ((f32[16,40,128]{2,1,0:T(8,128)}), f32[16,40,128]{2,1,0:T(8,128)S(1)}, u32[]{:S(2)}, u32[]{:S(2)}) async-start(f32[16,40,128]{2,1,0:T(8,128)} %shard_map.48), calls=%async_computation.5 | async-start | bytes 655360 | tf_op jit(solution)/shard_map/all_to_all | solution.py:16
  108.5 8.5 %all-to-all-start.6 = ((f32[4,32,128]{2,1,0:T(8,128)}), f32[4,32,128]{2,1,0:T(8,128)S(1)}, u32[]{:S(2)}, u32[]{:S(2)}) async-start(f32[4,32,128]{2,1,0:T(8,128)} %get-tuple-element.10), calls=%async_computation.6 | async-start | bytes 131072 | tf_op jit(solution)/shard_map/all_to_all | solution.py:16
  117.4 34.5 %copy-start.2 = (s32[96,1]{0,1:T(1,128)S(1)}, s32[96,1]{0,1:T(1,128)}, u32[]{:S(2)}) copy-start(s32[96,1]{0,1:T(1,128)} %param.7) | copy-start | bytes 1156
  148.3 13.5 %all-to-all-start.8 = ((f32[4,536,128]{2,1,0:T(8,128)}), f32[4,536,128]{2,1,0:T(8,128)S(1)}, u32[]{:S(2)}, u32[]{:S(2)}) async-start(f32[4,536,128]{2,1,0:T(8,128)} %shard_map.51), calls=%async_computation.8 | async-start | bytes 2195456 | tf_op jit(solution)/shard_map/all_to_all | solution.py:16
  161.9 13.5 %copy-start.1 = (f32[96,4096]{1,0:T(8,128)S(1)}, f32[96,4096]{1,0:T(8,128)}, u32[]{:S(2)}) copy-start(f32[96,4096]{1,0:T(8,128)} %corpus_ref.1) | copy-start | bytes 4718596
